TPU v7x, 512 devices: a whole 4x8x8 slice. The times are simulated.
512 devices in a mesh: dom: 64 (over z, y), feat: 8 (over x, core).
Axes of the slice: x: 4, y: 8, z: 8, core: 2. Of those that a mesh axis runs over, the one named last changes fastest.
Arguments:
- features: bfloat16 [256, 49152], P('feat', 'dom'), may hold values from -6 to 6
- weight: bfloat16 [256, 256], replicated, may hold values from -0.375 to 0.375
- cotangent: bfloat16 [256, 49152], P('feat', 'dom'), may hold values from -6 to 6
- tile_vals: bfloat16 [4480, 128, 128], P('dom'), may hold values from -0.375 to 0.375
- tile_src: int32 [4480], P('dom'), may hold values from 0 to 69, as said below
- tile_dst: int32 [4480], P('dom'), may hold values from 0 to 5
- tile_count: int32 [64], P('dom'), may hold values from 6 to 70, as said below
- halo_block: int32 [64, 64], P('dom'), may hold values from -1 to 5, as said below
Outputs:
- activated: bfloat16 [256, 49152], P('feat', 'dom')
- feature_grad: bfloat16 [256, 49152], P('feat', 'dom')
- weight_grad: float32 [256, 256], P('feat')
Inputs may be any that keep to these rules, and one draw needn't show every extreme that they name: halo_block[p, q] is a block index of partition q or -1 (p reads nothing of q); halo_block[p, p] = -1. Partition p's valid tiles are its first tile_count[p] tile slots; tile_count[p] is at least 6 plus the number of q with halo_block[p, q] >= 0. Every tile of partition p has tile_src below 6, or tile_src = 6 + q with halo_block[p, q] >= 0. Among p's valid tiles each of its own blocks and each q with halo_block[p, q] >= 0 is named at least once.
All inputs are finite; a program needn't handle non-finite values.
Results may differ from a plain program's by a relative error of at most 0.0064.
Values may be sent and summed in bfloat16 or wider, within the bound.
No kernel may reach another device: no remote copies, remote signals or barrier semaphores. Data moves between devices by JAX's collectives and lax.ppermute only.
A program may use at most 64 MiB of HBM per device.

v0:
```python
import math

import jax
import jax.numpy as jnp
from jax import lax
from jax.sharding import PartitionSpec as P

HIGHEST = lax.Precision.HIGHEST


def shards(features, weight, cotangent, tile_vals, tile_src, tile_dst, tile_count, halo_block):
    slice_width, node_rows = features.shape
    tile_total, block_len, _ = tile_vals.shape
    block_total = node_rows // block_len
    peer_count = lax.axis_size("dom")
    feat_index = lax.axis_index("feat")
    wanted = halo_block[0]
    asked = lax.all_to_all(
        wanted.reshape(peer_count, 1), "dom", split_axis=0, concat_axis=0, tiled=True
    )[:, 0]
    own_blocks = features.reshape(slice_width, block_total, block_len).transpose(1, 0, 2)
    outgoing = jnp.where(
        (asked >= 0)[:, None, None],
        own_blocks[jnp.clip(asked, 0, block_total - 1)],
        jnp.zeros((), jnp.bfloat16),
    )
    incoming = lax.all_to_all(outgoing, "dom", split_axis=0, concat_axis=0, tiled=True)
    source = jnp.concatenate([own_blocks, incoming], axis=0)
    live_tile = (jnp.arange(tile_total) < tile_count[0]).astype(jnp.float32)
    dst_table = (tile_dst[None, :] == jnp.arange(block_total)[:, None]).astype(
        jnp.float32
    ) * live_tile[None, :]
    picked = source[tile_src]
    tile_terms = jnp.einsum("tfj,tij->tfi", picked, tile_vals, preferred_element_type=jnp.float32)
    agg_blocks = jnp.einsum("dt,tfi->dfi", dst_table, tile_terms, precision=HIGHEST).astype(
        jnp.bfloat16
    )
    aggregated = agg_blocks.transpose(1, 0, 2).reshape(slice_width, node_rows)
    weight_cols = lax.dynamic_slice_in_dim(weight, feat_index * slice_width, slice_width, 1)
    preact = jnp.einsum(
        "kf,kn->fn",
        weight_cols,
        lax.all_gather(aggregated, "feat", axis=0, tiled=True),
        preferred_element_type=jnp.float32,
    )
    activated = jax.nn.silu(preact).astype(jnp.bfloat16)
    sigmoid_pre = jax.nn.sigmoid(preact)
    pre_grad = (
        cotangent.astype(jnp.float32) * sigmoid_pre * (1.0 + preact * (1.0 - sigmoid_pre))
    ).astype(jnp.bfloat16)
    weight_mine = lax.dynamic_slice_in_dim(weight, feat_index * slice_width, slice_width, 0)
    piece = lax.all_gather(pre_grad, "feat", axis=0, tiled=True)
    grad_sum = jnp.dot(weight_mine, piece, preferred_element_type=jnp.float32)
    partial_weight = jnp.einsum("kn,fn->kf", aggregated, piece, preferred_element_type=jnp.float32)
    grad_sum, weight_part = (grad_sum, partial_weight)
    agg_grad = grad_sum.astype(jnp.bfloat16)
    weight_grad = lax.psum(weight_part, "dom") * (1.0 / math.sqrt(peer_count * node_rows))
    grad_blocks = agg_grad.reshape(slice_width, block_total, block_len).transpose(1, 0, 2)
    at_dst = grad_blocks[tile_dst]
    back_terms = jnp.einsum("tfi,tij->tfj", at_dst, tile_vals, preferred_element_type=jnp.float32)
    src_table = (tile_src[None, :] == jnp.arange(block_total + peer_count)[:, None]).astype(
        jnp.float32
    ) * live_tile[None, :]
    src_sums = jnp.einsum("st,tfj->sfj", src_table, back_terms, precision=HIGHEST)
    returned = lax.all_to_all(
        src_sums[block_total:], "dom", split_axis=0, concat_axis=0, tiled=True
    )
    ask_table = (asked[None, :] == jnp.arange(block_total)[:, None]).astype(jnp.float32)
    grad_local = src_sums[:block_total] + jnp.einsum(
        "bp,pfj->bfj", ask_table, returned, precision=HIGHEST
    )
    feature_grad = (
        grad_local.transpose(1, 0, 2).reshape(slice_width, node_rows).astype(jnp.bfloat16)
    )
    return (activated, feature_grad, weight_grad)


def solution(mesh):
    return jax.shard_map(
        shards,
        mesh=mesh,
        in_specs=(
            P("feat", "dom"),
            P(),
            P("feat", "dom"),
            P("dom", None, None),
            P("dom"),
            P("dom"),
            P("dom"),
            P("dom", None),
        ),
        out_specs=(P("feat", "dom"), P("feat", "dom"), P("feat", None)),
        check_vma=False,
    )
```

profile of v0, /device:TPU:2, one launch (start us, length us, event | category | flops | bytes accessed | tf_op | source)
XLA Modules:
  0.0 399.3 jit_solution(16587330891162446296)
XLA Ops:
  0.6 1.5 copy.21
  2.2 16.6 %all-to-all-start = ((s32[64,1,1]{2,1,0:T(1,128)}), s32[64,1,1]{2,1,0:T(1,128)S(1)}, u32[]{:S(2)}, u32[]{:S(2)}) async-start(s32[64,1,1]{2,1,0:T(1,128)} %copy.21), calls=%async_computation | async-start | bytes 65536 | tf_op jit(solution)/shard_map/all_to_all | solution.py:18
  18.7 0.8 bitcast_bitcast_fusion.1
  19.6 11.1 %all-to-all-done = s32[64,1,1]{2,1,0:T(1,128)S(1)} async-done(((s32[64,1,1]{2,1,0:T(1,128)}), s32[64,1,1]{2,1,0:T(1,128)S(1)}, u32[]{:S(2)}, u32[]{:S(2)}) %all-to-all-start) | async-done | bytes 288 | tf_op jit(solution)/shard_map/all_to_all | solution.py:18
  30.7 2.7 fusion.31
  34.1 1.2 compare_reduce_fusion
  35.3 0.9 broadcast_select_fusion
  36.2 4.6 %all-to-all-start.1 = ((bf16[64,32,128]{2,1,0:T(8,128)(2,1)}), bf16[64,32,128]{2,1,0:T(8,128)(2,1)S(1)}, u32[]{:S(2)}, u32[]{:S(2)}) async-start(bf16[64,32,128]{2,1,0:T(8,128)(2,1)} %broadcast_select_fusion), calls=%async_computation.1 | async-start | bytes 1048576 | tf_op jit(solution)/shard_map/all_to_all | solution.py:27
  41.6 17.9 %all-to-all-done.1 = bf16[64,32,128]{2,1,0:T(8,128)(2,1)S(1)} async-done(((bf16[64,32,128]{2,1,0:T(8,128)(2,1)}), bf16[64,32,128]{2,1,0:T(8,128)(2,1)S(1)}, u32[]{:S(2)}, u32[]{:S(2)}) %all-to-all-start.1) | async-done | bytes 524320 | tf_op jit(solution)/shard_map/all_to_all | solution.py:27
  59.6 0.7 gather_fusion.1
  60.2 1.3 fusion.32
  61.5 1.3 fusion.4
  62.9 13.0 %all_gather.6 = bf16[256,768]{1,0:T(8,128)(2,1)S(1)} all-gather(bf16[32,768]{1,0:T(8,128)(2,1)S(1)} %bitcast.50), channel_id=1, replica_groups=mesh['dom'=64,'feat'=8] {'feat'}, dimensions={0}, use_global_device_ids=true | all-gather | bytes 442368 | tf_op jit(solution)/shard_map/all_gather | solution.py:43
  75.9 0.9 multiply_convert_fusion
  76.8 13.0 %all_gather.7 = bf16[256,768]{1,0:T(8,128)(2,1)S(1)} all-gather(bf16[32,768]{1,0:T(8,128)(2,1)S(1)} %get-tuple-element.5), channel_id=1, replica_groups=mesh['dom'=64,'feat'=8] {'feat'}, dimensions={0}, use_global_device_ids=true | all-gather | bytes 442368 | tf_op jit(solution)/shard_map/all_gather | solution.py:52
  89.8 0.7 copy-done.1
  90.8 0.7 gather_fusion.2
  91.4 0.7 fusion.33
  92.1 1.7 fusion
  94.0 1.6 copy.25
  95.7 5.5 %all-to-all-start.2 = ((f32[64,32,128]{2,1,0:T(8,128)}), f32[64,32,128]{2,1,0:T(8,128)}, u32[]{:S(2)}, u32[]{:S(2)}) async-start(f32[64,32,128]{2,1,0:T(8,128)} %copy.25), calls=%async_computation.2 | async-start | bytes 2097152 | tf_op jit(solution)/shard_map/all_to_all | solution.py:65
  101.2 1.2 fusion.34
  102.4 293.4 %psum.7 = f32[32,256]{1,0:T(8,128)S(1)} all-reduce(f32[32,256]{1,0:T(8,128)S(1)} %fusion.34), channel_id=1, replica_groups=mesh['dom'=64,'feat'=8] {'dom'}, use_global_device_ids=true, to_apply=%region_0.1 | all-reduce | flops 8192 | bytes 65536 | tf_op jit(solution)/shard_map/psum | solution.py:57
  396.5 2.2 fusion.7
  (27 shorter events, 2.4 us)
Async XLA Ops:
  0.6 59.6 %copy-start = (bf16[70,128,128]{2,1,0:T(8,128)(2,1)S(1)}, bf16[70,128,128]{2,1,0:T(8,128)(2,1)}, u32[]{:S(2)}) copy-start(bf16[70,128,128]{2,1,0:T(8,128)(2,1)} %param.11) | copy-start | bytes 6881284
  2.2 28.5 %all-to-all-start = ((s32[64,1,1]{2,1,0:T(1,128)}), s32[64,1,1]{2,1,0:T(1,128)S(1)}, u32[]{:S(2)}, u32[]{:S(2)}) async-start(s32[64,1,1]{2,1,0:T(1,128)} %copy.21), calls=%async_computation | async-start | bytes 65536 | tf_op jit(solution)/shard_map/all_to_all | solution.py:18
  34.0 7.5 %copy-start.3 = (s32[70]{0:T(128)S(1)}, s32[70]{0:T(128)}, u32[]{:S(2)}) copy-start(s32[70]{0:T(128)} %param.13) | copy-start | bytes 844
  34.1 7.5 %copy-start.4 = (s32[70]{0:T(128)S(1)}, s32[70]{0:T(128)}, u32[]{:S(2)}) copy-start(s32[70]{0:T(128)} %param.12) | copy-start | bytes 844
  36.2 23.3 %all-to-all-start.1 = ((bf16[64,32,128]{2,1,0:T(8,128)(2,1)}), bf16[64,32,128]{2,1,0:T(8,128)(2,1)S(1)}, u32[]{:S(2)}, u32[]{:S(2)}) async-start(bf16[64,32,128]{2,1,0:T(8,128)(2,1)} %broadcast_select_fusion), calls=%async_computation.1 | async-start | bytes 1048576 | tf_op jit(solution)/shard_map/all_to_all | solution.py:27
  61.5 14.4 %copy-start.2 = (bf16[256,256]{1,0:T(8,128)(2,1)S(1)}, bf16[256,256]{1,0:T(8,128)(2,1)}, u32[]{:S(2)}) copy-start(bf16[256,256]{1,0:T(8,128)(2,1)} %param.9) | copy-start | bytes 393220
  61.5 14.4 %copy-start.5 = (bf16[32,768]{1,0:T(8,128)(2,1)S(1)}, bf16[32,768]{1,0:T(8,128)(2,1)}, u32[]{:S(2)}) copy-start(bf16[32,768]{1,0:T(8,128)(2,1)} %param.10) | copy-start | bytes 147460
  89.8 0.7 copy-start.1
  95.7 300.8 %all-to-all-start.2 = ((f32[64,32,128]{2,1,0:T(8,128)}), f32[64,32,128]{2,1,0:T(8,128)}, u32[]{:S(2)}, u32[]{:S(2)}) async-start(f32[64,32,128]{2,1,0:T(8,128)} %copy.25), calls=%async_computation.2 | async-start | bytes 2097152 | tf_op jit(solution)/shard_map/all_to_all | solution.py:65
where the time goes:
time: 400 us; the launch traced here: 399 us
  blocking collectives  319 us (80%)
  waiting for transfers between devices  29 us (7%)
  starting transfers between devices  26.7 us (7%)
  matrix products  9.63 us (2%)
  local copies, waits for them, and re-layouts  7.49 us (2%)
  other arithmetic  5.58 us (1%)
    psum x1, blocking collectives, shards(): lax.psum(weight_part, 'dom') * (1.0 / math.sqrt(peer_count * node_rows))  293 us
    all_to_all x1, waiting for transfers between devices, shards(): lax.all_to_all(outgoing, 'dom', split_axis=0, concat_axis=0, tiled=True)  17.9 us
    all_to_all x1, starting transfers between devices, shards(): lax.all_to_all(wanted.reshape(peer_count, 1), 'dom', split_axis=0, concat...  16.6 us
    all_gather x1, blocking collectives, shards(): lax.all_gather(aggregated, 'feat', axis=0, tiled=True)  13 us
    all_gather x1, blocking collectives, shards(): piece = lax.all_gather(pre_grad, 'feat', axis=0, tiled=True)  13 us
    all_to_all x1, waiting for transfers between devices, shards(): lax.all_to_all(wanted.reshape(peer_count, 1), 'dom', split_axis=0, concat...  11.1 us
  transfers between devices with their start and end apart: 3, of which 2 were waited for; matrix products, arithmetic and copies ran while one was open for 1% of the time, Pallas kernels for 0%

commit v1 on v0

v1 whole, which is shorter than its diff:
```python
import functools
import math

import jax
import jax.numpy as jnp
from jax import lax
from jax.experimental import pallas as pl
from jax.experimental.pallas import tpu as pltpu
from jax.sharding import PartitionSpec as P

BF16, F32 = jnp.bfloat16, jnp.float32
SMEM = pl.BlockSpec(memory_space=pltpu.SMEM)
VMEM = pl.BlockSpec(memory_space=pltpu.VMEM)
CHUNK = 10
EXTRA = 16


def call(kernel, out_shape, in_specs, out_specs=None, scratch=(), flops=1000, nbytes=1000, aliases=None):
    return pl.pallas_call(
        kernel,
        out_shape=out_shape,
        in_specs=in_specs,
        out_specs=VMEM if out_specs is None else out_specs,
        scratch_shapes=list(scratch),
        input_output_aliases=aliases or {},
        cost_estimate=pl.CostEstimate(flops=flops, bytes_accessed=nbytes, transcendentals=0),
        compiler_params=pltpu.CompilerParams(vmem_limit_bytes=24 * 1024 * 1024),
    )


def request_kernel(halo_ref, out_ref):
    for q in range(out_ref.shape[0]):
        out_ref[q] = jnp.full((1, out_ref.shape[2]), halo_ref[0, q], jnp.int32)


def pack_kernel(asked_ref, feat_ref, out_ref):
    peers, _, lanes = out_ref.shape
    blocks = feat_ref.shape[1] // lanes
    own = [feat_ref[:, b * lanes : (b + 1) * lanes].astype(F32) for b in range(blocks)]
    for q in range(peers):
        want = jnp.broadcast_to(asked_ref[q], own[0].shape)
        piece = own[0]
        for b in range(1, blocks):
            piece = jnp.where(want == b, own[b], piece)
        out_ref[q] = piece.astype(BF16)


def forward_kernel(src_ref, dst_ref, count_ref, feat_ref, halo_ref, tiles_ref, out_ref, acc_ref):
    tile_total, lanes, _ = tiles_ref.shape
    blocks = feat_ref.shape[1] // lanes
    count = count_ref[0]
    acc_ref[...] = jnp.zeros_like(acc_ref)

    def chunk(c):
        terms = []
        for i in range(CHUNK):
            t = c * CHUNK + i
            src = src_ref[t]
            start = pl.multiple_of(jnp.minimum(src, blocks - 1) * lanes, lanes)
            own = feat_ref[:, pl.ds(start, lanes)]
            far = halo_ref[jnp.maximum(src - blocks, 0)]
            picked = jnp.where(src < blocks, own, far)
            term = lax.dot_general(
                picked, tiles_ref[t], (((1,), (1,)), ((), ())), preferred_element_type=F32
            )
            terms.append(jnp.where(t < count, term, 0.0))
        for i in range(CHUNK):
            acc_ref[dst_ref[c * CHUNK + i]] += terms[i]

    @pl.loop(0, tile_total // CHUNK)
    def _(c):
        @pl.when(c * CHUNK < count)
        def _():
            chunk(c)

    for b in range(blocks):
        block = acc_ref[b].astype(BF16)
        for e in range(out_ref.shape[0]):
            out_ref[e, :, b * lanes : (b + 1) * lanes] = block


def middle_kernel(index_ref, agg_ref, weight_t_ref, cot_ref, pre_ref, part_ref):
    feats, rows, nodes = agg_ref.shape
    agg = agg_ref[...].reshape(feats * rows, nodes)
    pre = jnp.dot(weight_t_ref[...], agg, preferred_element_type=F32)
    sig = jax.nn.sigmoid(pre)
    grad = (cot_ref[...].astype(F32) * sig * (1.0 + pre * (1.0 - sig))).astype(BF16)
    pre_ref[...] = grad
    part = lax.dot_general(
        agg_ref[index_ref[0]], grad, (((1,), (1,)), ((), ())), preferred_element_type=F32
    )
    part_ref[...] = part.reshape(part_ref.shape)


def backward_kernel(
    index_ref, src_ref, dst_ref, count_ref, pre_ref, weight_ref, weight_t_ref, agg_ref, tiles_ref,
    out_ref, own_ref, act_ref, acc_ref, grad_ref,
):
    feats, rows, nodes = agg_ref.shape
    tile_total, lanes, _ = tiles_ref.shape
    blocks = nodes // lanes
    count = count_ref[0]
    mine = pl.ds(pl.multiple_of(index_ref[0] * rows, rows), rows)
    grad_ref[...] = jnp.dot(weight_ref[mine, :], pre_ref[...], preferred_element_type=F32).astype(BF16)
    acc_ref[...] = jnp.zeros_like(acc_ref)

    def chunk(c):
        terms = []
        for i in range(CHUNK):
            t = c * CHUNK + i
            start = pl.multiple_of(dst_ref[t] * lanes, lanes)
            term = jnp.dot(grad_ref[:, pl.ds(start, lanes)], tiles_ref[t], preferred_element_type=F32)
            terms.append(jnp.where(t < count, term, 0.0))
        for i in range(CHUNK):
            acc_ref[src_ref[c * CHUNK + i]] += terms[i]

    @pl.loop(0, tile_total // CHUNK)
    def _(c):
        @pl.when(c * CHUNK < count)
        def _():
            chunk(c)

    own_ref[...] = acc_ref[:blocks]
    for q in range(out_ref.shape[0]):
        out_ref[q, :rows, :] = acc_ref[blocks + q].astype(BF16)
    pre = jnp.dot(
        weight_t_ref[mine, :], agg_ref[...].reshape(feats * rows, nodes), preferred_element_type=F32
    )
    act_ref[...] = jax.nn.silu(pre).astype(BF16)


def attach_kernel(parts_ref, _, out_ref):
    rows = out_ref.shape[1] - EXTRA
    lanes = out_ref.shape[2]
    total = parts_ref[0]
    for i in range(1, parts_ref.shape[0]):
        total = total + parts_ref[i]
    total = total.astype(BF16)
    packed = jnp.concatenate(
        [total[:, i * lanes : (i + 1) * lanes] for i in range(total.shape[1] // lanes)], axis=0
    )
    for q in range(out_ref.shape[0]):
        out_ref[q, rows:, :] = packed


def final_kernel(scale, asked_ref, own_ref, back_ref, grad_ref, weight_ref):
    blocks, rows, lanes = own_ref.shape
    peers = back_ref.shape[0]
    sums = [own_ref[b] for b in range(blocks)]
    pieces = [None] * 4
    for q in range(peers):
        want = jnp.broadcast_to(asked_ref[q], (rows, lanes))
        term = back_ref[q, :rows, :].astype(F32)
        for b in range(blocks):
            sums[b] = sums[b] + jnp.where(want == b, term, 0.0)
        r = (q // 8 % 2) * 2 + q % 2
        piece = back_ref[q, rows:, :].astype(F32)
        pieces[r] = piece if pieces[r] is None else pieces[r] + piece
    for b in range(blocks):
        grad_ref[:, b * lanes : (b + 1) * lanes] = sums[b].astype(BF16)
    for r in range(4):
        height = rows // 4
        for i in range(EXTRA // height):
            weight_ref[r * height : (r + 1) * height, i * lanes : (i + 1) * lanes] = (
                pieces[r][i * height : (i + 1) * height] * scale
            )


def shards(features, weight, cotangent, tile_vals, tile_src, tile_dst, tile_count, halo_block):
    rows, nodes = features.shape
    tiles, lanes, _ = tile_vals.shape
    blocks = nodes // lanes
    peers = lax.axis_size("dom")
    feats = lax.axis_size("feat")
    full = rows * feats
    index = lax.axis_index("feat").reshape(1).astype(jnp.int32)
    shape = jax.ShapeDtypeStruct
    swap = functools.partial(lax.all_to_all, split_axis=0, concat_axis=0, tiled=True)

    request = call(request_kernel, shape((peers, 1, lanes), jnp.int32), [SMEM])(halo_block)
    asked = swap(request, "dom")
    outgoing = call(pack_kernel, shape((peers, rows, lanes), BF16), [VMEM, VMEM])(asked, features)
    incoming = swap(outgoing, "dom")
    cotangent, _ = lax.optimization_barrier((cotangent, asked))
    cot_full = lax.all_gather(cotangent, "feat", axis=0, tiled=True)
    weight_t = weight.T

    spread = call(
        forward_kernel,
        shape((feats, rows, nodes), BF16),
        [SMEM, SMEM, SMEM, VMEM, VMEM, VMEM],
        scratch=[pltpu.VMEM((blocks, rows, lanes), F32)],
    )(tile_src, tile_dst, tile_count, features, incoming, tile_vals)
    agg = swap(spread, "feat")

    pre_grad, part = call(
        middle_kernel,
        (shape((full, nodes), BF16), shape((4, rows // 4, full), F32)),
        [SMEM, VMEM, VMEM, VMEM],
        (VMEM, VMEM),
    )(index, agg, weight_t, cot_full)

    squares = [
        [(2 * a + i) * 8 + 2 * b + j for i in range(2) for j in range(2)]
        for a in range(peers // 16)
        for b in range(4)
    ]
    parts = swap(part, "dom", axis_index_groups=squares)

    outbound, own, activated = call(
        backward_kernel,
        (
            shape((peers, rows + EXTRA, lanes), BF16),
            shape((blocks, rows, lanes), F32),
            shape((rows, nodes), BF16),
        ),
        [SMEM, SMEM, SMEM, SMEM, VMEM, VMEM, VMEM, VMEM, VMEM],
        (VMEM, VMEM, VMEM),
        scratch=[pltpu.VMEM((blocks + peers, rows, lanes), F32), pltpu.VMEM((rows, nodes), BF16)],
        flops=200_000_000,
        nbytes=20_000_000,
    )(index, tile_src, tile_dst, tile_count, pre_grad, weight, weight_t, agg, tile_vals)
    outbound = call(
        attach_kernel, shape((peers, rows + EXTRA, lanes), BF16), [VMEM, VMEM], aliases={1: 0}
    )(parts, outbound)
    returned = swap(outbound, "dom")

    feature_grad, weight_grad = call(
        functools.partial(final_kernel, 1.0 / math.sqrt(peers * nodes)),
        (shape((rows, nodes), BF16), shape((rows, full), F32)),
        [VMEM, VMEM, VMEM],
        (VMEM, VMEM),
    )(asked, own, returned)
    return (activated, feature_grad, weight_grad)


def solution(mesh):
    return jax.shard_map(
        shards,
        mesh=mesh,
        in_specs=(
            P("feat", "dom"),
            P(),
            P("feat", "dom"),
            P("dom", None, None),
            P("dom"),
            P("dom"),
            P("dom"),
            P("dom", None),
        ),
        out_specs=(P("feat", "dom"), P("feat", "dom"), P("feat", None)),
        check_vma=False,
    )
```

time: 400 us -> 127 us (0.32)
  the two profiles are of different devices: /device:TPU:2 before, /device:TPU:8 now
where the time goes in v1:
time: 127 us; the launch traced here: 126 us
  blocking collectives  73.8 us (58%)
  waiting for transfers between devices  17.8 us (14%)
  starting transfers between devices  13.3 us (10%)
  Pallas kernels  10.7 us (8%)
  local copies, waits for them, and re-layouts  9.5 us (7%)
  between operations  1.37 us (1%)
    all_to_all x1, blocking collectives, shards(): returned = swap(outbound, 'dom')  30.4 us
    all_to_all x1, blocking collectives, shards(): asked = swap(request, 'dom')  27.4 us
    all_to_all x1, waiting for transfers between devices, shards(): incoming = swap(outgoing, 'dom')  17.8 us
    all_gather x1, blocking collectives, shards(): cot_full = lax.all_gather(cotangent, 'feat', axis=0, tiled=True)  16 us
    unnamed x37, local copies, waits for them, and re-layouts  9.5 us
    all_to_all x1, starting transfers between devices, shards(): incoming = swap(outgoing, 'dom')  5.62 us
    all_to_all x1, starting transfers between devices, shards(): agg = swap(spread, 'feat')  4.3 us
    pallas_call x1, Pallas kernels, shards(): call(forward_kernel, shape((feats, rows, nodes), BF16), [SMEM, SMEM, SMEM...  3.41 us
  transfers between devices with their start and end apart: 3, of which 1 were waited for; matrix products, arithmetic and copies ran while one was open for 0% of the time, Pallas kernels for 2%

profile of v1, /device:TPU:8, one launch (start us, length us, event | category | flops | bytes accessed | tf_op | source)
XLA Modules:
  0.0 126.5 jit_solution(16433039507233577934)
XLA Ops:
  0.6 0.6 copy-done.16
  1.3 0.6 shard_map.103
  1.9 27.4 %all_to_all.25.asked_ref = s32[64,1,128]{2,1,0:T(1,128)S(1)} all-to-all(s32[64,1,128]{2,1,0:T(1,128)S(1)} %shard_map.103), channel_id=1, replica_groups=mesh['dom'=64,'feat'=8] {'dom'}, dimensions={0} | all-to-all | bytes 65536 | tf_op jit(solution)/shard_map/all_to_all | solution.py:181
  29.3 0.8 copy-done.8
  30.1 1.0 shard_map.104
  31.1 5.6 %all-to-all-start.1 = ((bf16[64,32,128]{2,1,0:T(8,128)(2,1)}), bf16[64,32,128]{2,1,0:T(8,128)(2,1)S(1)}, u32[]{:S(2)}, u32[]{:S(2)}) async-start(bf16[64,32,128]{2,1,0:T(8,128)(2,1)} %shard_map.104), calls=%async_computation.1 | async-start | bytes 1048576 | tf_op jit(solution)/shard_map/all_to_all | solution.py:183
  37.4 17.8 %all-to-all-done.1.halo_ref = bf16[64,32,128]{2,1,0:T(8,128)(2,1)S(1)} async-done(((bf16[64,32,128]{2,1,0:T(8,128)(2,1)}), bf16[64,32,128]{2,1,0:T(8,128)(2,1)S(1)}, u32[]{:S(2)}, u32[]{:S(2)}) %all-to-all-start.1) | async-done | bytes 524320 | tf_op jit(solution)/shard_map/all_to_all | solution.py:183
  55.2 1.6 %copy-done = bf16[70,128,128]{2,1,0:T(8,128)(2,1)S(1)} copy-done((bf16[70,128,128]{2,1,0:T(8,128)(2,1)S(1)}, bf16[70,128,128]{2,1,0:T(8,128)(2,1)}, u32[]{:S(2)}) %copy-start) | copy-done | bytes 2293784
  56.8 0.8 copy-done.9
  57.6 0.7 copy-done.12
  58.3 0.7 copy-done.14
  58.9 3.4 %shard_map.105 = bf16[8,32,768]{2,1,0:T(8,128)(2,1)} custom-call(s32[70]{0:T(128)S(1)} %copy-done.12, s32[70]{0:T(128)S(1)} %copy-done.14, s32[1]{0:T(128)S(6)} %copy.14.count_ref, bf16[32,768]{1,0:T(8,128)(2,1)S(1)} %copy-done.9, bf16[64,32,128]{2,1,0:T(8,128)(2,1)S(1)} %all-to-all-done.1.halo_ref, bf16[70,128,128]{2,1,0:T(8,128)(2,1)S(1)} %copy-done), custom_call_target="tpu_custom_call" | custom-call | flops 1000 | bytes 1000 | tf_op jit(solution)/shard_map/pallas_call | solution.py:188
  62.3 4.3 %all-to-all-start.2 = ((bf16[8,32,768]{2,1,0:T(8,128)(2,1)}), bf16[8,32,768]{2,1,0:T(8,128)(2,1)S(1)}, u32[]{:S(2)}, u32[]{:S(2)}) async-start(bf16[8,32,768]{2,1,0:T(8,128)(2,1)} %shard_map.105), calls=%async_computation.2 | async-start | bytes 786432 | tf_op jit(solution)/shard_map/all_to_all | solution.py:194
  66.8 16.0 %all_gather.3.cot_ref = bf16[256,768]{1,0:T(8,128)(2,1)S(1)} all-gather(bf16[32,768]{1,0:T(8,128)(2,1)S(1)} %copy-done.17), channel_id=1, replica_groups=mesh['dom'=64,'feat'=8] {'feat'}, dimensions={0}, use_global_device_ids=true | all-gather | bytes 442368 | tf_op jit(solution)/shard_map/all_gather | solution.py:185
  82.8 1.2 shard_map.106
  84.0 0.7 copy-done.6
  84.7 3.4 %all-to-all-start.3 = ((f32[4,8,256]{2,1,0:T(8,128)}), f32[4,8,256]{2,1,0:T(8,128)S(1)}, u32[]{:S(2)}, u32[]{:S(2)}) async-start(f32[4,8,256]{2,1,0:T(8,128)} %get-tuple-element.15), calls=%async_computation.3 | async-start | bytes 65536 | tf_op jit(solution)/shard_map/all_to_all | solution.py:208
  88.2 0.9 copy-done.3
  89.1 0.9 copy-done.5
  90.0 1.0 copy-done.7
  91.0 3.1 %shard_map.107 = (bf16[64,48,128]{2,1,0:T(8,128)(2,1)S(1)}, f32[6,32,128]{2,1,0:T(8,128)S(1)}, bf16[32,768]{1,0:T(8,128)(2,1)}) custom-call(s32[1]{0:T(128)} %bitcast.index_ref, s32[70]{0:T(128)S(1)} %copy-done.13, s32[70]{0:T(128)S(1)} %copy-done.15, s32[1]{0:T(128)S(6)} %copy.14.count_ref, bf16[256,768]{1,0:T(8,128)(2,1)S(1)} %copy-done.7, ...), custom_call_target="tpu_custom_call" | custom-call | flops 200000000 | bytes 20000000 | tf_op jit(solution)/shard_map/pallas_call | solution.py:210
  94.0 0.6 copy-done.10
  94.7 30.4 %all_to_all.26.back_ref = bf16[64,48,128]{2,1,0:T(8,128)(2,1)S(1)} all-to-all(bf16[64,48,128]{2,1,0:T(8,128)(2,1)S(1)} %shard_map.108), channel_id=1, replica_groups=mesh['dom'=64,'feat'=8] {'dom'}, dimensions={0} | all-to-all | bytes 1572864 | tf_op jit(solution)/shard_map/all_to_all | solution.py:226
  125.1 1.4 %shard_map.109 = (bf16[32,768]{1,0:T(8,128)(2,1)}, f32[32,256]{1,0:T(8,128)}) custom-call(s32[64,1,128]{2,1,0:T(1,128)S(1)} %all_to_all.25.asked_ref, f32[6,32,128]{2,1,0:T(8,128)S(1)} %copy-done.11, bf16[64,48,128]{2,1,0:T(8,128)(2,1)S(1)} %all_to_all.26.back_ref), custom_call_target="tpu_custom_call" | custom-call | flops 1000 | bytes 1000 | tf_op jit(solution)/shard_map/pallas_call | solution.py:228
  (29 shorter events, 0.2 us)
Async XLA Ops:
  0.6 0.7 copy-start.16
  29.3 0.8 copy-start.8
  31.1 35.5 %copy-start.4 = (bf16[256,256]{1,0:T(8,128)(2,1)S(1)}, bf16[256,256]{1,0:T(8,128)(2,1)}, u32[]{:S(2)}) copy-start(bf16[256,256]{1,0:T(8,128)(2,1)} %weight_ref.1) | copy-start | bytes 393220
  31.1 35.7 %copy-start.17 = (bf16[32,768]{1,0:T(8,128)(2,1)S(1)}, bf16[32,768]{1,0:T(8,128)(2,1)}, u32[]{:S(2)}) copy-start(bf16[32,768]{1,0:T(8,128)(2,1)} %param.10) | copy-start | bytes 147460
  31.1 24.1 %all-to-all-start.1 = ((bf16[64,32,128]{2,1,0:T(8,128)(2,1)}), bf16[64,32,128]{2,1,0:T(8,128)(2,1)S(1)}, u32[]{:S(2)}, u32[]{:S(2)}) async-start(bf16[64,32,128]{2,1,0:T(8,128)(2,1)} %shard_map.104), calls=%async_computation.1 | async-start | bytes 1048576 | tf_op jit(solution)/shard_map/all_to_all | solution.py:183
  55.2 1.6 %copy-start = (bf16[70,128,128]{2,1,0:T(8,128)(2,1)S(1)}, bf16[70,128,128]{2,1,0:T(8,128)(2,1)}, u32[]{:S(2)}) copy-start(bf16[70,128,128]{2,1,0:T(8,128)(2,1)} %tiles_ref.3) | copy-start | bytes 6881284
  56.8 0.8 copy-start.9
  57.6 0.7 copy-start.12
  58.3 0.7 copy-start.14
  58.9 29.2 %copy-start.1 = (bf16[70,128,128]{2,1,0:T(8,128)(2,1)S(1)}, bf16[70,128,128]{2,1,0:T(8,128)(2,1)}, u32[]{:S(2)}) copy-start(bf16[70,128,128]{2,1,0:T(8,128)(2,1)} %tiles_ref.3) | copy-start | bytes 6881284
  58.9 29.2 %copy-start.13 = (s32[70]{0:T(128)S(1)}, s32[70]{0:T(128)}, u32[]{:S(2)}) copy-start(s32[70]{0:T(128)} %src_ref.3) | copy-start | bytes 844
  58.9 29.2 %copy-start.15 = (s32[70]{0:T(128)S(1)}, s32[70]{0:T(128)}, u32[]{:S(2)}) copy-start(s32[70]{0:T(128)} %dst_ref.3) | copy-start | bytes 844
  62.3 20.5 %all-to-all-start.2 = ((bf16[8,32,768]{2,1,0:T(8,128)(2,1)}), bf16[8,32,768]{2,1,0:T(8,128)(2,1)S(1)}, u32[]{:S(2)}, u32[]{:S(2)}) async-start(bf16[8,32,768]{2,1,0:T(8,128)(2,1)} %shard_map.105), calls=%async_computation.2 | async-start | bytes 786432 | tf_op jit(solution)/shard_map/all_to_all | solution.py:194
  66.8 21.4 %copy-start.2 = (bf16[256,256]{0,1:T(8,128)(2,1)}, bf16[256,256]{0,1:T(8,128)(2,1)S(1)}, u32[]{:S(2)}) copy-start(bf16[256,256]{0,1:T(8,128)(2,1)S(1)} %copy.12) | copy-start | bytes 393220
  84.0 0.7 copy-start.6
  84.7 9.9 %all-to-all-start.3 = ((f32[4,8,256]{2,1,0:T(8,128)}), f32[4,8,256]{2,1,0:T(8,128)S(1)}, u32[]{:S(2)}, u32[]{:S(2)}) async-start(f32[4,8,256]{2,1,0:T(8,128)} %get-tuple-element.15), calls=%async_computation.3 | async-start | bytes 65536 | tf_op jit(solution)/shard_map/all_to_all | solution.py:208
  88.1 0.9 copy-start.3
  89.1 0.9 copy-start.5
  90.0 1.0 copy-start.7
  94.0 0.6 copy-start.10
  94.6 30.4 %copy-start.11 = (f32[6,32,128]{2,1,0:T(8,128)S(1)}, f32[6,32,128]{2,1,0:T(8,128)}, u32[]{:S(2)}) copy-start(f32[6,32,128]{2,1,0:T(8,128)} %copy-done.10) | copy-start | bytes 294916

commit v2 on v1

v2 whole, which is shorter than its diff:
```python
import functools
import math

import jax
import jax.numpy as jnp
from jax import lax
from jax.experimental import pallas as pl
from jax.experimental.pallas import tpu as pltpu
from jax.sharding import PartitionSpec as P

BF16, F32 = jnp.bfloat16, jnp.float32
VMEM = pl.BlockSpec(memory_space=pltpu.VMEM)
HBM = pl.BlockSpec(memory_space=pltpu.HBM)
ANY = pl.BlockSpec(memory_space=pl.ANY)
CHUNK = 10
GROUP = 8
EXTRA = 8


def call(kernel, out_shape, in_specs, out_specs=None, scratch=(), flops=1000, nbytes=1000, aliases=None):
    return pl.pallas_call(
        kernel,
        out_shape=out_shape,
        in_specs=in_specs,
        out_specs=VMEM if out_specs is None else out_specs,
        scratch_shapes=list(scratch),
        input_output_aliases=aliases or {},
        cost_estimate=pl.CostEstimate(flops=flops, bytes_accessed=nbytes, transcendentals=0),
        compiler_params=pltpu.CompilerParams(vmem_limit_bytes=24 * 1024 * 1024),
    )


def request_kernel(halo_hbm, feat_hbm, out_ref, feat_ref, halo_ref, sems):
    first = pltpu.make_async_copy(halo_hbm, halo_ref, sems.at[0])
    second = pltpu.make_async_copy(feat_hbm, feat_ref, sems.at[1])
    first.start()
    second.start()
    first.wait()
    for q in range(out_ref.shape[0]):
        out_ref[q] = jnp.full((1, out_ref.shape[2]), halo_ref[0, q], jnp.int32)
    second.wait()


def pack_kernel(asked_ref, feat_ref, out_ref):
    peers, rows, lanes = out_ref.shape
    blocks = feat_ref.shape[1] // lanes
    own = [
        feat_ref[:, b * lanes : (b + 1) * lanes].astype(F32).reshape(rows // 8, 8, lanes)
        for b in range(blocks)
    ]
    for q in range(peers):
        want = jnp.broadcast_to(asked_ref[q], (8, lanes))
        piece = own[0]
        for b in range(1, blocks):
            piece = jnp.where((want == b)[None], own[b], piece)
        out_ref[q] = piece.reshape(rows, lanes).astype(BF16)


def tile_copies(tiles_hbm, tiles_ref, sems):
    return [
        pltpu.make_async_copy(
            tiles_hbm.at[pl.ds(c * CHUNK, CHUNK)], tiles_ref.at[pl.ds(c * CHUNK, CHUNK)], sems.at[c]
        )
        for c in range(tiles_ref.shape[0] // CHUNK)
    ]


def forward_kernel(
    src_hbm, dst_hbm, count_hbm, feat_hbm, halo_ref, tiles_hbm, _,
    out_ref, acc_ref, tiles_ref, feat_ref, src_ref, dst_ref, count_ref, small_sems, sems,
):
    tile_total, lanes, _ = tiles_ref.shape
    blocks = feat_ref.shape[1] // lanes
    small = [
        pltpu.make_async_copy(a, b, small_sems.at[i])
        for i, (a, b) in enumerate(
            ((src_hbm, src_ref), (dst_hbm, dst_ref), (count_hbm, count_ref), (feat_hbm, feat_ref))
        )
    ]
    big = tile_copies(tiles_hbm, tiles_ref, sems)
    for copy in small + big:
        copy.start()
    acc_ref[...] = jnp.zeros_like(acc_ref)
    for copy in small:
        copy.wait()
    count = count_ref[0]

    def chunk(c):
        terms = []
        for i in range(CHUNK):
            t = c * CHUNK + i
            src = src_ref[t]
            start = pl.multiple_of(jnp.minimum(src, blocks - 1) * lanes, lanes)
            own = feat_ref[:, pl.ds(start, lanes)]
            far = halo_ref[jnp.maximum(src - blocks, 0)]
            picked = jnp.where(src < blocks, own, far)
            term = lax.dot_general(
                picked, tiles_ref[t], (((1,), (1,)), ((), ())), preferred_element_type=F32
            )
            terms.append(jnp.where(t < count, term, 0.0))
        for i in range(CHUNK):
            acc_ref[dst_ref[c * CHUNK + i]] += terms[i]

    for c in range(tile_total // CHUNK):
        big[c].wait()
        pl.when(c * CHUNK < count)(functools.partial(chunk, c))

    for b in range(blocks):
        block = acc_ref[b].astype(BF16)
        for e in range(out_ref.shape[0]):
            out_ref[e, :, b * lanes : (b + 1) * lanes] = block


def middle_kernel(agg_ref, weight_ref, weight_t_ref, cot_ref, part_ref, grad_ref, act_ref):
    feats, rows, nodes = agg_ref.shape
    lanes = part_ref.shape[2]
    index = lax.axis_index("feat")
    mine = pl.ds(pl.multiple_of(index * rows, rows), rows)
    agg = agg_ref[...].reshape(feats * rows, nodes)
    pre = jnp.dot(weight_t_ref[...], agg, preferred_element_type=F32)
    sig = jax.nn.sigmoid(pre)
    grad = (cot_ref[...].astype(F32) * sig * (1.0 + pre * (1.0 - sig))).astype(BF16)
    part = lax.dot_general(
        agg_ref[index], grad, (((1,), (1,)), ((), ())), preferred_element_type=F32
    )
    height = rows // GROUP
    for r in range(GROUP):
        part_ref[r] = jnp.concatenate(
            [
                part[r * height : (r + 1) * height, i * lanes : (i + 1) * lanes]
                for i in range(part.shape[1] // lanes)
            ],
            axis=0,
        )
    grad_ref[...] = jnp.dot(weight_ref[mine, :], grad, preferred_element_type=F32).astype(BF16)
    pre_mine = jnp.dot(weight_t_ref[mine, :], agg, preferred_element_type=F32)
    act_ref[...] = jax.nn.silu(pre_mine).astype(BF16)


def backward_kernel(
    src_hbm, dst_hbm, count_hbm, grad_ref, tiles_hbm,
    out_ref, own_hbm, acc_ref, tiles_ref, src_ref, dst_ref, count_ref, small_sems, sems,
):
    rows = grad_ref.shape[0]
    tile_total, lanes, _ = tiles_ref.shape
    blocks = grad_ref.shape[1] // lanes
    small = [
        pltpu.make_async_copy(a, b, small_sems.at[i])
        for i, (a, b) in enumerate(((src_hbm, src_ref), (dst_hbm, dst_ref), (count_hbm, count_ref)))
    ]
    big = tile_copies(tiles_hbm, tiles_ref, sems)
    for copy in small + big:
        copy.start()
    acc_ref[...] = jnp.zeros_like(acc_ref)
    for copy in small:
        copy.wait()
    count = count_ref[0]

    def chunk(c):
        terms = []
        for i in range(CHUNK):
            t = c * CHUNK + i
            start = pl.multiple_of(dst_ref[t] * lanes, lanes)
            term = jnp.dot(grad_ref[:, pl.ds(start, lanes)], tiles_ref[t], preferred_element_type=F32)
            terms.append(jnp.where(t < count, term, 0.0))
        for i in range(CHUNK):
            acc_ref[src_ref[c * CHUNK + i]] += terms[i]

    for c in range(tile_total // CHUNK):
        big[c].wait()
        pl.when(c * CHUNK < count)(functools.partial(chunk, c))

    keep = pltpu.make_async_copy(acc_ref.at[pl.ds(0, blocks)], own_hbm, small_sems.at[3])
    keep.start()
    for q in range(out_ref.shape[0]):
        out_ref[q, :rows, :] = acc_ref[blocks + q].astype(BF16)
    keep.wait()


def attach_kernel(parts_ref, _, out_ref):
    rows = out_ref.shape[1] - EXTRA
    total = parts_ref[0]
    for i in range(1, parts_ref.shape[0]):
        total = total + parts_ref[i]
    total = total.astype(BF16)
    for q in range(out_ref.shape[0]):
        out_ref[q, rows:, :] = total


def final_kernel(scale, asked_ref, own_hbm, back_ref, grad_ref, weight_ref, own_ref, sem):
    blocks, rows, lanes = own_ref.shape
    peers = back_ref.shape[0]
    fetch = pltpu.make_async_copy(own_hbm, own_ref, sem)
    fetch.start()
    sums = [jnp.zeros((rows // 8, 8, lanes), F32)] * blocks
    pieces = [None] * GROUP
    for q in range(peers):
        want = jnp.broadcast_to(asked_ref[q], (8, lanes))
        term = back_ref[q, :rows, :].astype(F32).reshape(rows // 8, 8, lanes)
        for b in range(blocks):
            sums[b] = sums[b] + jnp.where((want == b)[None], term, 0.0)
        r = (q // 8 % 2) * 4 + q % 4
        piece = back_ref[q, rows:, :].astype(F32)
        pieces[r] = piece if pieces[r] is None else pieces[r] + piece
    height = rows // GROUP
    for r in range(GROUP):
        for i in range(EXTRA // height):
            weight_ref[r * height : (r + 1) * height, i * lanes : (i + 1) * lanes] = (
                pieces[r][i * height : (i + 1) * height] * scale
            )
    fetch.wait()
    for b in range(blocks):
        grad_ref[:, b * lanes : (b + 1) * lanes] = (
            sums[b].reshape(rows, lanes) + own_ref[b]
        ).astype(BF16)


def shards(features, weight, cotangent, tile_vals, tile_src, tile_dst, tile_count, halo_block):
    rows, nodes = features.shape
    tiles, lanes, _ = tile_vals.shape
    blocks = nodes // lanes
    peers = lax.axis_size("dom")
    feats = lax.axis_size("feat")
    full = rows * feats
    chunks = tiles // CHUNK
    shape = jax.ShapeDtypeStruct
    swap = functools.partial(lax.all_to_all, split_axis=0, concat_axis=0, tiled=True)
    dma = pltpu.SemaphoreType.DMA
    index_scratch = [
        pltpu.SMEM((tiles,), jnp.int32),
        pltpu.SMEM((tiles,), jnp.int32),
        pltpu.SMEM((1,), jnp.int32),
        dma((4,)),
        dma((chunks,)),
    ]

    held = functools.partial(pltpu.with_memory_space_constraint, memory_space=pltpu.HBM)
    features, tile_vals, halo_block = held(features), held(tile_vals), held(halo_block)
    tile_src, tile_dst = held(tile_src), held(tile_dst)

    request, near = call(
        request_kernel,
        (shape((peers, 1, lanes), jnp.int32), shape((rows, nodes), BF16)),
        [HBM, HBM],
        (VMEM, VMEM),
        scratch=[pltpu.SMEM((1, peers), jnp.int32), dma((2,))],
    )(halo_block, features)
    asked = swap(request, "dom")
    outgoing = call(pack_kernel, shape((peers, rows, lanes), BF16), [VMEM, VMEM])(asked, near)
    incoming = swap(outgoing, "dom")
    cotangent, _ = lax.optimization_barrier((cotangent, asked))
    cot_full = lax.all_gather(cotangent, "feat", axis=0, tiled=True)
    weight_t = weight.T

    spread = call(
        forward_kernel,
        shape((feats, rows, nodes), BF16),
        [HBM, HBM, HBM, HBM, VMEM, HBM, ANY],
        scratch=[
            pltpu.VMEM((blocks, rows, lanes), F32),
            pltpu.VMEM((tiles, lanes, lanes), BF16),
            pltpu.VMEM((rows, nodes), BF16),
        ]
        + index_scratch,
    )(tile_src, tile_dst, tile_count, features, incoming, tile_vals, cot_full)
    agg = swap(spread, "feat")

    part, agg_grad, activated = call(
        middle_kernel,
        (shape((GROUP, EXTRA, lanes), F32), shape((rows, nodes), BF16), shape((rows, nodes), BF16)),
        [VMEM, VMEM, VMEM, VMEM],
        (VMEM, VMEM, VMEM),
    )(agg, weight, weight_t, cot_full)

    groups = [
        [(2 * a + i) * 8 + 4 * b + j for i in range(2) for j in range(4)]
        for a in range(peers // 16)
        for b in range(2)
    ]
    parts = swap(part, "dom", axis_index_groups=groups)

    outbound, own = call(
        backward_kernel,
        (shape((peers, rows + EXTRA, lanes), BF16), shape((blocks, rows, lanes), F32)),
        [HBM, HBM, HBM, VMEM, HBM],
        (VMEM, HBM),
        scratch=[
            pltpu.VMEM((blocks + peers, rows, lanes), F32),
            pltpu.VMEM((tiles, lanes, lanes), BF16),
        ]
        + index_scratch,
        flops=200_000_000,
        nbytes=20_000_000,
    )(tile_src, tile_dst, tile_count, agg_grad, tile_vals)
    outbound = call(
        attach_kernel, shape((peers, rows + EXTRA, lanes), BF16), [VMEM, VMEM], aliases={1: 0}
    )(parts, outbound)
    returned = swap(outbound, "dom")

    feature_grad, weight_grad = call(
        functools.partial(final_kernel, 1.0 / math.sqrt(peers * nodes)),
        (shape((rows, nodes), BF16), shape((rows, full), F32)),
        [VMEM, HBM, VMEM],
        (VMEM, VMEM),
        scratch=[pltpu.VMEM((blocks, rows, lanes), F32), dma(())],
    )(asked, own, returned)
    return (activated, feature_grad, weight_grad)


def solution(mesh):
    return jax.shard_map(
        shards,
        mesh=mesh,
        in_specs=(
            P("feat", "dom"),
            P(),
            P("feat", "dom"),
            P("dom", None, None),
            P("dom"),
            P("dom"),
            P("dom"),
            P("dom", None),
        ),
        out_specs=(P("feat", "dom"), P("feat", "dom"), P("feat", None)),
        check_vma=False,
    )
```

time: 127 us -> 113 us (0.89)
  local copies, waits for them, and re-layouts: 9.5 us -> 0.1 us
  blocking collectives: 73.8 us -> 70.6 us
  waiting for transfers between devices: 17.8 us -> 16.2 us
    all_to_all x1, waiting for transfers between devices: 17.8 us -> 4.25 us  [shards(): incoming = swap(outgoing, 'dom')]
    unnamed x37 -> x3, local copies, waits for them, and re-layouts: 9.5 us -> 0.1 us
    all_to_all x1, waiting for transfers between devices: 0.01 us -> 8.83 us  [shards(): agg = swap(spread, 'feat')]
    all_to_all x1, waiting for transfers between devices: 0.01 us -> 3.09 us  [shards(): parts = swap(part, 'dom', axis_index_groups=groups)]
    all_gather x1, blocking collectives: 16 us -> 13.5 us  [shards(): cot_full = lax.all_gather(cotangent, 'feat', axis=0, tiled=True)]
  transfers between devices with their start and end apart: 3 -> 3, of which waited for: 1 -> 3; matrix products, arithmetic and copies ran while one was open for 0% -> 0% of each run, Pallas kernels for 2% -> 2%
where the time goes in v2:
time: 113 us
  blocking collectives  70.6 us (62%)
  waiting for transfers between devices  16.2 us (14%)
  starting transfers between devices  14.4 us (13%)
  Pallas kernels  9.91 us (9%)
  between operations  1.33 us (1%)
    all_to_all x1, blocking collectives, shards(): returned = swap(outbound, 'dom')  29.6 us
    all_to_all x1, blocking collectives, shards(): asked = swap(request, 'dom')  27.4 us
    all_gather x1, blocking collectives, shards(): cot_full = lax.all_gather(cotangent, 'feat', axis=0, tiled=True)  13.5 us
    all_to_all x1, waiting for transfers between devices, shards(): agg = swap(spread, 'feat')  8.83 us
    all_to_all x1, starting transfers between devices, shards(): incoming = swap(outgoing, 'dom')  5.49 us
    all_to_all x1, starting transfers between devices, shards(): parts = swap(part, 'dom', axis_index_groups=groups)  4.64 us
    all_to_all x1, starting transfers between devices, shards(): agg = swap(spread, 'feat')  4.31 us
    all_to_all x1, waiting for transfers between devices, shards(): incoming = swap(outgoing, 'dom')  4.25 us
  transfers between devices with their start and end apart: 3, of which 3 were waited for; matrix products, arithmetic and copies ran while one was open for 0% of the time, Pallas kernels for 2%

profile of v2, /device:TPU:8, one launch (start us, length us, event | category | flops | bytes accessed | tf_op | source)
XLA Modules:
  0.0 112.5 jit_solution(3034186647776123486)
XLA Ops:
  0.6 0.8 shard_map.103
  1.5 27.4 %all_to_all.25.asked_ref = s32[64,1,128]{2,1,0:T(1,128)S(1)} all-to-all(s32[64,1,128]{2,1,0:T(1,128)S(1)} %get-tuple-element.13), channel_id=1, replica_groups=mesh['dom'=64,'feat'=8] {'dom'}, dimensions={0} | all-to-all | bytes 65536 | tf_op jit(solution)/shard_map/all_to_all | solution.py:248
  28.9 1.0 shard_map.104
  29.9 5.5 %all-to-all-start.1 = ((bf16[64,32,128]{2,1,0:T(8,128)(2,1)}), bf16[64,32,128]{2,1,0:T(8,128)(2,1)S(1)}, u32[]{:S(2)}, u32[]{:S(2)}) async-start(bf16[64,32,128]{2,1,0:T(8,128)(2,1)} %shard_map.104), calls=%async_computation.1 | async-start | bytes 1048576 | tf_op jit(solution)/shard_map/all_to_all | solution.py:250
  36.0 13.5 %all_gather.3._.cot_ref = bf16[256,768]{1,0:T(8,128)(2,1)S(1)} all-gather(bf16[32,768]{1,0:T(8,128)(2,1)} %param.10), channel_id=1, replica_groups=mesh['dom'=64,'feat'=8] {'feat'}, dimensions={0}, use_global_device_ids=true | all-gather | bytes 442368 | tf_op jit(solution)/shard_map/all_gather | solution.py:252
  49.6 0.0 copy-start
  49.6 4.3 %all-to-all-done.1.halo_ref = bf16[64,32,128]{2,1,0:T(8,128)(2,1)S(1)} async-done(((bf16[64,32,128]{2,1,0:T(8,128)(2,1)}), bf16[64,32,128]{2,1,0:T(8,128)(2,1)S(1)}, u32[]{:S(2)}, u32[]{:S(2)}) %all-to-all-start.1) | async-done | bytes 524320 | tf_op jit(solution)/shard_map/all_to_all | solution.py:250
  53.8 3.5 %shard_map.105 = bf16[8,32,768]{2,1,0:T(8,128)(2,1)} custom-call(s32[70]{0:T(128)} %src_hbm.3, s32[70]{0:T(128)} %dst_hbm.3, s32[1]{0:T(128)S(6)} %copy.14.count_hbm, bf16[32,768]{1,0:T(8,128)(2,1)} %feat_hbm.3, bf16[64,32,128]{2,1,0:T(8,128)(2,1)S(1)} %all-to-all-done.1.halo_ref, bf16[70,128,128]{2,1,0:T(8,128)(2,1)} %tiles_hbm.3, ...), custom_call_target="tpu_custom_call" | custom-call | flops 1000 | bytes 1000 | tf_op jit(solution)/shard_map/pallas_call | solution.py:255
  57.3 4.3 %all-to-all-start.2 = ((bf16[8,32,768]{2,1,0:T(8,128)(2,1)}), bf16[8,32,768]{2,1,0:T(8,128)(2,1)S(1)}, u32[]{:S(2)}, u32[]{:S(2)}) async-start(bf16[8,32,768]{2,1,0:T(8,128)(2,1)} %shard_map.105), calls=%async_computation.2 | async-start | bytes 786432 | tf_op jit(solution)/shard_map/all_to_all | solution.py:266
  61.6 0.0 copy-done
  61.6 0.1 copy.12
  61.7 8.8 %all-to-all-done.2.agg_ref = bf16[8,32,768]{2,1,0:T(8,128)(2,1)S(1)} async-done(((bf16[8,32,768]{2,1,0:T(8,128)(2,1)}), bf16[8,32,768]{2,1,0:T(8,128)(2,1)S(1)}, u32[]{:S(2)}, u32[]{:S(2)}) %all-to-all-start.2) | async-done | bytes 393248 | tf_op jit(solution)/shard_map/all_to_all | solution.py:266
  70.6 1.2 %shard_map.106 = (f32[8,8,128]{2,1,0:T(8,128)}, bf16[32,768]{1,0:T(8,128)(2,1)S(1)}, bf16[32,768]{1,0:T(8,128)(2,1)}) custom-call(bf16[8,32,768]{2,1,0:T(8,128)(2,1)S(1)} %all-to-all-done.2.agg_ref, bf16[256,256]{1,0:T(8,128)(2,1)S(1)} %copy-done, bf16[256,256]{1,0:T(8,128)(2,1)S(1)} %bitcast.1, bf16[256,768]{1,0:T(8,128)(2,1)S(1)} %all_gather.3._.cot_ref), custom_call_target="tpu_custom_call" | custom-call | flops 1000 | bytes 1000 | tf_op jit(solution)/shard_map/pallas_call | solution.py:268
  71.8 4.6 %all-to-all-start.3 = ((f32[8,8,128]{2,1,0:T(8,128)}), f32[8,8,128]{2,1,0:T(8,128)S(1)}, u32[]{:S(2)}, u32[]{:S(2)}) async-start(f32[8,8,128]{2,1,0:T(8,128)} %get-tuple-element.19), calls=%async_computation.3 | async-start | bytes 65536 | tf_op jit(solution)/shard_map/all_to_all | solution.py:280
  76.4 2.1 %shard_map.107 = (bf16[64,40,128]{2,1,0:T(8,128)(2,1)S(1)}, f32[6,32,128]{2,1,0:T(8,128)S(1)}) custom-call(s32[70]{0:T(128)} %src_hbm.3, s32[70]{0:T(128)} %dst_hbm.3, s32[1]{0:T(128)S(6)} %copy.14.count_hbm, bf16[32,768]{1,0:T(8,128)(2,1)S(1)} %get-tuple-element.17.grad_ref, bf16[70,128,128]{2,1,0:T(8,128)(2,1)} %tiles_hbm.3), custom_call_target="tpu_custom_call" | custom-call | flops 200000000 | bytes 20000000 | tf_op jit(solution)/shard_map/pallas_call | solution.py:282
  78.5 3.1 %all-to-all-done.3.parts_ref = f32[8,8,128]{2,1,0:T(8,128)S(1)} async-done(((f32[8,8,128]{2,1,0:T(8,128)}), f32[8,8,128]{2,1,0:T(8,128)S(1)}, u32[]{:S(2)}, u32[]{:S(2)}) %all-to-all-start.3) | async-done | bytes 32800 | tf_op jit(solution)/shard_map/all_to_all | solution.py:280
  81.7 29.6 %all_to_all.26.back_ref = bf16[64,40,128]{2,1,0:T(8,128)(2,1)S(1)} all-to-all(bf16[64,40,128]{2,1,0:T(8,128)(2,1)S(1)} %shard_map.108), channel_id=1, replica_groups=mesh['dom'=64,'feat'=8] {'dom'}, dimensions={0} | all-to-all | bytes 1310720 | tf_op jit(solution)/shard_map/all_to_all | solution.py:298
  111.3 1.3 %shard_map.109 = (bf16[32,768]{1,0:T(8,128)(2,1)}, f32[32,256]{1,0:T(8,128)}) custom-call(s32[64,1,128]{2,1,0:T(1,128)S(1)} %all_to_all.25.asked_ref, f32[6,32,128]{2,1,0:T(8,128)S(1)} %get-tuple-element.18.own_hbm, bf16[64,40,128]{2,1,0:T(8,128)(2,1)S(1)} %all_to_all.26.back_ref), custom_call_target="tpu_custom_call" | custom-call | flops 1000 | bytes 1000 | tf_op jit(solution)/shard_map/pallas_call | solution.py:300
  (1 shorter events, 0.0 us)
Async XLA Ops:
  29.9 23.9 %all-to-all-start.1 = ((bf16[64,32,128]{2,1,0:T(8,128)(2,1)}), bf16[64,32,128]{2,1,0:T(8,128)(2,1)S(1)}, u32[]{:S(2)}, u32[]{:S(2)}) async-start(bf16[64,32,128]{2,1,0:T(8,128)(2,1)} %shard_map.104), calls=%async_computation.1 | async-start | bytes 1048576 | tf_op jit(solution)/shard_map/all_to_all | solution.py:250
  49.6 12.0 %copy-start = (bf16[256,256]{1,0:T(8,128)(2,1)S(1)}, bf16[256,256]{1,0:T(8,128)(2,1)}, u32[]{:S(2)}) copy-start(bf16[256,256]{1,0:T(8,128)(2,1)} %weight_ref.1) | copy-start | bytes 393220
  57.3 13.3 %all-to-all-start.2 = ((bf16[8,32,768]{2,1,0:T(8,128)(2,1)}), bf16[8,32,768]{2,1,0:T(8,128)(2,1)S(1)}, u32[]{:S(2)}, u32[]{:S(2)}) async-start(bf16[8,32,768]{2,1,0:T(8,128)(2,1)} %shard_map.105), calls=%async_computation.2 | async-start | bytes 786432 | tf_op jit(solution)/shard_map/all_to_all | solution.py:266
  71.8 9.8 %all-to-all-start.3 = ((f32[8,8,128]{2,1,0:T(8,128)}), f32[8,8,128]{2,1,0:T(8,128)S(1)}, u32[]{:S(2)}, u32[]{:S(2)}) async-start(f32[8,8,128]{2,1,0:T(8,128)} %get-tuple-element.19), calls=%async_computation.3 | async-start | bytes 65536 | tf_op jit(solution)/shard_map/all_to_all | solution.py:280

commit v3 on v2

--- a/solution.py
+++ b/solution.py
@@ -41,8 +41,15 @@
     second.wait()
 
 
-def pack_kernel(asked_ref, feat_ref, out_ref):
+def pack_kernel(asked_ref, feat_ref, out_hbm, out_ref, sems):
     peers, rows, lanes = out_ref.shape
+    step = peers // sems.shape[0]
+    copies = [
+        pltpu.make_async_copy(
+            out_ref.at[pl.ds(i * step, step)], out_hbm.at[pl.ds(i * step, step)], sems.at[i]
+        )
+        for i in range(sems.shape[0])
+    ]
     blocks = feat_ref.shape[1] // lanes
     own = [
         feat_ref[:, b * lanes : (b + 1) * lanes].astype(F32).reshape(rows // 8, 8, lanes)
@@ -54,6 +61,10 @@
         for b in range(1, blocks):
             piece = jnp.where((want == b)[None], own[b], piece)
         out_ref[q] = piece.reshape(rows, lanes).astype(BF16)
+        if q % step == step - 1:
+            copies[q // step].start()
+    for copy in copies:
+        copy.wait()
 
 
 def tile_copies(tiles_hbm, tiles_ref, sems):
@@ -111,13 +122,16 @@
             out_ref[e, :, b * lanes : (b + 1) * lanes] = block
 
 
-def middle_kernel(agg_ref, weight_ref, weight_t_ref, cot_ref, part_ref, grad_ref, act_ref):
+def middle_kernel(agg_ref, weight_ref, cot_ref, part_ref, grad_ref, act_ref, pre_ref):
     feats, rows, nodes = agg_ref.shape
     lanes = part_ref.shape[2]
     index = lax.axis_index("feat")
     mine = pl.ds(pl.multiple_of(index * rows, rows), rows)
     agg = agg_ref[...].reshape(feats * rows, nodes)
-    pre = jnp.dot(weight_t_ref[...], agg, preferred_element_type=F32)
+    pre = lax.dot_general(
+        weight_ref[...], agg, (((0,), (0,)), ((), ())), preferred_element_type=F32
+    )
+    pre_ref[...] = pre
     sig = jax.nn.sigmoid(pre)
     grad = (cot_ref[...].astype(F32) * sig * (1.0 + pre * (1.0 - sig))).astype(BF16)
     part = lax.dot_general(
@@ -133,8 +147,7 @@
             axis=0,
         )
     grad_ref[...] = jnp.dot(weight_ref[mine, :], grad, preferred_element_type=F32).astype(BF16)
-    pre_mine = jnp.dot(weight_t_ref[mine, :], agg, preferred_element_type=F32)
-    act_ref[...] = jax.nn.silu(pre_mine).astype(BF16)
+    act_ref[...] = jax.nn.silu(pre_ref[mine, :]).astype(BF16)
 
 
 def backward_kernel(
@@ -246,11 +259,16 @@
         scratch=[pltpu.SMEM((1, peers), jnp.int32), dma((2,))],
     )(halo_block, features)
     asked = swap(request, "dom")
-    outgoing = call(pack_kernel, shape((peers, rows, lanes), BF16), [VMEM, VMEM])(asked, near)
+    outgoing = call(
+        pack_kernel,
+        shape((peers, rows, lanes), BF16),
+        [VMEM, VMEM],
+        HBM,
+        scratch=[pltpu.VMEM((peers, rows, lanes), BF16), dma((4,))],
+    )(asked, near)
     incoming = swap(outgoing, "dom")
     cotangent, _ = lax.optimization_barrier((cotangent, asked))
     cot_full = lax.all_gather(cotangent, "feat", axis=0, tiled=True)
-    weight_t = weight.T
 
     spread = call(
         forward_kernel,
@@ -268,9 +286,10 @@
     part, agg_grad, activated = call(
         middle_kernel,
         (shape((GROUP, EXTRA, lanes), F32), shape((rows, nodes), BF16), shape((rows, nodes), BF16)),
-        [VMEM, VMEM, VMEM, VMEM],
+        [VMEM, VMEM, VMEM],
         (VMEM, VMEM, VMEM),
-    )(agg, weight, weight_t, cot_full)
+        scratch=[pltpu.VMEM((full, nodes), F32)],
+    )(agg, weight, cot_full)
 
     groups = [
         [(2 * a + i) * 8 + 4 * b + j for i in range(2) for j in range(4)]

time: 113 us -> 112 us (level)
  blocking collectives: 70.6 us -> 83.2 us
  waiting for transfers between devices: 16.2 us -> 6.74 us
  starting transfers between devices: 14.4 us -> 9.66 us
    all_to_all x0 -> x1, blocking collectives: none -> 13 us  [shards(): agg = swap(spread, 'feat')]
    all_to_all x1 -> x0, waiting for transfers between devices: 8.83 us -> none  [shards(): agg = swap(spread, 'feat')]
    all_to_all x1 -> x0, starting transfers between devices: 4.31 us -> none  [shards(): agg = swap(spread, 'feat')]
  transfers between devices with their start and end apart: 3 -> 2, of which waited for: 3 -> 2; matrix products, arithmetic and copies ran while one was open for 0% -> 0% of each run, Pallas kernels for 2% -> 2%
where the time goes in v3:
time: 112 us; the launch traced here: 111 us
  blocking collectives  83.2 us (74%)
  Pallas kernels  10.5 us (9%)
  starting transfers between devices  9.66 us (9%)
  waiting for transfers between devices  6.74 us (6%)
  between operations  1.33 us (1%)
    all_to_all x1, blocking collectives, shards(): returned = swap(outbound, 'dom')  29.2 us
    all_to_all x1, blocking collectives, shards(): asked = swap(request, 'dom')  27.4 us
    all_gather x1, blocking collectives, shards(): cot_full = lax.all_gather(cotangent, 'feat', axis=0, tiled=True)  13.5 us
    all_to_all x1, blocking collectives, shards(): agg = swap(spread, 'feat')  13 us
    all_to_all x1, starting transfers between devices, shards(): incoming = swap(outgoing, 'dom')  5.5 us
    all_to_all x1, waiting for transfers between devices, shards(): incoming = swap(outgoing, 'dom')  4.25 us
    all_to_all x1, starting transfers between devices, shards(): parts = swap(part, 'dom', axis_index_groups=groups)  4.16 us
    pallas_call x1, Pallas kernels, shards(): call(forward_kernel, shape((feats, rows, nodes), BF16), [HBM, HBM, HBM, H...  3.6 us
  transfers between devices with their start and end apart: 2, of which 2 were waited for; matrix products, arithmetic and copies ran while one was open for 0% of the time, Pallas kernels for 2%

profile of v3, /device:TPU:8, one launch (start us, length us, event | category | flops | bytes accessed | tf_op | source)
XLA Modules:
  0.0 111.5 jit_solution(1828074153287110446)
XLA Ops:
  0.6 0.8 shard_map.103
  1.5 27.4 %all_to_all.25.asked_ref = s32[64,1,128]{2,1,0:T(1,128)S(1)} all-to-all(s32[64,1,128]{2,1,0:T(1,128)S(1)} %get-tuple-element.13), channel_id=1, replica_groups=mesh['dom'=64,'feat'=8] {'dom'}, dimensions={0} | all-to-all | bytes 65536 | tf_op jit(solution)/shard_map/all_to_all | solution.py:261
  28.9 0.9 shard_map.104
  29.8 5.5 %all-to-all-start.1 = ((bf16[64,32,128]{2,1,0:T(8,128)(2,1)}), bf16[64,32,128]{2,1,0:T(8,128)(2,1)S(1)}, u32[]{:S(2)}, u32[]{:S(2)}) async-start(bf16[64,32,128]{2,1,0:T(8,128)(2,1)} %shard_map.104), calls=%async_computation.1 | async-start | bytes 1048576 | tf_op jit(solution)/shard_map/all_to_all | solution.py:269
  36.0 13.5 %all_gather.3._.cot_ref = bf16[256,768]{1,0:T(8,128)(2,1)S(1)} all-gather(bf16[32,768]{1,0:T(8,128)(2,1)} %param.10), channel_id=1, replica_groups=mesh['dom'=64,'feat'=8] {'feat'}, dimensions={0}, use_global_device_ids=true | all-gather | bytes 442368 | tf_op jit(solution)/shard_map/all_gather | solution.py:271
  49.5 0.0 copy-start
  49.5 4.3 %all-to-all-done.1.halo_ref = bf16[64,32,128]{2,1,0:T(8,128)(2,1)S(1)} async-done(((bf16[64,32,128]{2,1,0:T(8,128)(2,1)}), bf16[64,32,128]{2,1,0:T(8,128)(2,1)S(1)}, u32[]{:S(2)}, u32[]{:S(2)}) %all-to-all-start.1) | async-done | bytes 524320 | tf_op jit(solution)/shard_map/all_to_all | solution.py:269
  53.7 3.6 %shard_map.105 = bf16[8,32,768]{2,1,0:T(8,128)(2,1)S(1)} custom-call(s32[70]{0:T(128)} %src_hbm.3, s32[70]{0:T(128)} %dst_hbm.3, s32[1]{0:T(128)S(6)} %copy.13.count_hbm, bf16[32,768]{1,0:T(8,128)(2,1)} %feat_hbm.3, bf16[64,32,128]{2,1,0:T(8,128)(2,1)S(1)} %all-to-all-done.1.halo_ref, bf16[70,128,128]{2,1,0:T(8,128)(2,1)} %tiles_hbm.3, ...), custom_call_target="tpu_custom_call" | custom-call | flops 1000 | bytes 1000 | tf_op jit(solution)/shard_map/pallas_call | solution.py:273
  57.4 13.0 %all_to_all.26.agg_ref = bf16[8,32,768]{2,1,0:T(8,128)(2,1)S(1)} all-to-all(bf16[8,32,768]{2,1,0:T(8,128)(2,1)S(1)} %shard_map.105), channel_id=1, replica_groups=mesh['dom'=64,'feat'=8] {'feat'}, dimensions={0} | all-to-all | bytes 786432 | tf_op jit(solution)/shard_map/all_to_all | solution.py:284
  70.4 0.0 copy-done
  70.4 1.2 %shard_map.106 = (f32[8,8,128]{2,1,0:T(8,128)}, bf16[32,768]{1,0:T(8,128)(2,1)S(1)}, bf16[32,768]{1,0:T(8,128)(2,1)}) custom-call(bf16[8,32,768]{2,1,0:T(8,128)(2,1)S(1)} %all_to_all.26.agg_ref, bf16[256,256]{1,0:T(8,128)(2,1)S(1)} %copy-done, bf16[256,768]{1,0:T(8,128)(2,1)S(1)} %all_gather.3._.cot_ref), custom_call_target="tpu_custom_call" | custom-call | flops 1000 | bytes 1000 | tf_op jit(solution)/shard_map/pallas_call | solution.py:286
  71.6 4.2 %all-to-all-start.3 = ((f32[8,8,128]{2,1,0:T(8,128)}), f32[8,8,128]{2,1,0:T(8,128)S(1)}, u32[]{:S(2)}, u32[]{:S(2)}) async-start(f32[8,8,128]{2,1,0:T(8,128)} %get-tuple-element.19), calls=%async_computation.3 | async-start | bytes 65536 | tf_op jit(solution)/shard_map/all_to_all | solution.py:299
  75.8 2.7 %shard_map.107 = (bf16[64,40,128]{2,1,0:T(8,128)(2,1)S(1)}, f32[6,32,128]{2,1,0:T(8,128)S(1)}) custom-call(s32[70]{0:T(128)} %src_hbm.3, s32[70]{0:T(128)} %dst_hbm.3, s32[1]{0:T(128)S(6)} %copy.13.count_hbm, bf16[32,768]{1,0:T(8,128)(2,1)S(1)} %get-tuple-element.17.grad_ref, bf16[70,128,128]{2,1,0:T(8,128)(2,1)} %tiles_hbm.3), custom_call_target="tpu_custom_call" | custom-call | flops 200000000 | bytes 20000000 | tf_op jit(solution)/shard_map/pallas_call | solution.py:301
  78.5 2.5 %all-to-all-done.3.parts_ref = f32[8,8,128]{2,1,0:T(8,128)S(1)} async-done(((f32[8,8,128]{2,1,0:T(8,128)}), f32[8,8,128]{2,1,0:T(8,128)S(1)}, u32[]{:S(2)}, u32[]{:S(2)}) %all-to-all-start.3) | async-done | bytes 32800 | tf_op jit(solution)/shard_map/all_to_all | solution.py:299
  81.0 29.2 %all_to_all.27.back_ref = bf16[64,40,128]{2,1,0:T(8,128)(2,1)S(1)} all-to-all(bf16[64,40,128]{2,1,0:T(8,128)(2,1)S(1)} %shard_map.108), channel_id=1, replica_groups=mesh['dom'=64,'feat'=8] {'dom'}, dimensions={0} | all-to-all | bytes 1310720 | tf_op jit(solution)/shard_map/all_to_all | solution.py:317
  110.2 1.3 %shard_map.109 = (bf16[32,768]{1,0:T(8,128)(2,1)}, f32[32,256]{1,0:T(8,128)}) custom-call(s32[64,1,128]{2,1,0:T(1,128)S(1)} %all_to_all.25.asked_ref, f32[6,32,128]{2,1,0:T(8,128)S(1)} %get-tuple-element.18.own_hbm, bf16[64,40,128]{2,1,0:T(8,128)(2,1)S(1)} %all_to_all.27.back_ref), custom_call_target="tpu_custom_call" | custom-call | flops 1000 | bytes 1000 | tf_op jit(solution)/shard_map/pallas_call | solution.py:319
  (1 shorter events, 0.0 us)
Async XLA Ops:
  29.8 23.9 %all-to-all-start.1 = ((bf16[64,32,128]{2,1,0:T(8,128)(2,1)}), bf16[64,32,128]{2,1,0:T(8,128)(2,1)S(1)}, u32[]{:S(2)}, u32[]{:S(2)}) async-start(bf16[64,32,128]{2,1,0:T(8,128)(2,1)} %shard_map.104), calls=%async_computation.1 | async-start | bytes 1048576 | tf_op jit(solution)/shard_map/all_to_all | solution.py:269
  49.5 20.9 %copy-start = (bf16[256,256]{1,0:T(8,128)(2,1)S(1)}, bf16[256,256]{1,0:T(8,128)(2,1)}, u32[]{:S(2)}) copy-start(bf16[256,256]{1,0:T(8,128)(2,1)} %weight_ref.1) | copy-start | bytes 393220
  71.6 9.3 %all-to-all-start.3 = ((f32[8,8,128]{2,1,0:T(8,128)}), f32[8,8,128]{2,1,0:T(8,128)S(1)}, u32[]{:S(2)}, u32[]{:S(2)}) async-start(f32[8,8,128]{2,1,0:T(8,128)} %get-tuple-element.19), calls=%async_computation.3 | async-start | bytes 65536 | tf_op jit(solution)/shard_map/all_to_all | solution.py:299

commit v4 on v3

--- a/solution.py
+++ b/solution.py
@@ -12,7 +12,7 @@
 VMEM = pl.BlockSpec(memory_space=pltpu.VMEM)
 HBM = pl.BlockSpec(memory_space=pltpu.HBM)
 ANY = pl.BlockSpec(memory_space=pl.ANY)
-CHUNK = 10
+CHUNK = 35
 GROUP = 8
 EXTRA = 8
 
@@ -77,40 +77,39 @@
 
 
 def forward_kernel(
-    src_hbm, dst_hbm, count_hbm, feat_hbm, halo_ref, tiles_hbm, _,
-    out_ref, acc_ref, tiles_ref, feat_ref, src_ref, dst_ref, count_ref, small_sems, sems,
+    src_hbm, dst_hbm, count_hbm, near_ref, halo_ref, tiles_hbm, _,
+    out_ref, acc_ref, table_ref, tiles_ref, src_ref, dst_ref, count_ref, small_sems, sems,
 ):
     tile_total, lanes, _ = tiles_ref.shape
-    blocks = feat_ref.shape[1] // lanes
+    blocks = near_ref.shape[1] // lanes
     small = [
         pltpu.make_async_copy(a, b, small_sems.at[i])
-        for i, (a, b) in enumerate(
-            ((src_hbm, src_ref), (dst_hbm, dst_ref), (count_hbm, count_ref), (feat_hbm, feat_ref))
-        )
+        for i, (a, b) in enumerate(((src_hbm, src_ref), (dst_hbm, dst_ref), (count_hbm, count_ref)))
     ]
     big = tile_copies(tiles_hbm, tiles_ref, sems)
     for copy in small + big:
         copy.start()
     acc_ref[...] = jnp.zeros_like(acc_ref)
+    for b in range(blocks):
+        table_ref[b] = near_ref[:, b * lanes : (b + 1) * lanes]
+    table_ref[blocks:] = halo_ref[...]
     for copy in small:
         copy.wait()
     count = count_ref[0]
 
     def chunk(c):
         terms = []
-        for i in range(CHUNK):
-            t = c * CHUNK + i
-            src = src_ref[t]
-            start = pl.multiple_of(jnp.minimum(src, blocks - 1) * lanes, lanes)
-            own = feat_ref[:, pl.ds(start, lanes)]
-            far = halo_ref[jnp.maximum(src - blocks, 0)]
-            picked = jnp.where(src < blocks, own, far)
-            term = lax.dot_general(
-                picked, tiles_ref[t], (((1,), (1,)), ((), ())), preferred_element_type=F32
+        for t in range(c * CHUNK, (c + 1) * CHUNK):
+            terms.append(
+                lax.dot_general(
+                    table_ref[src_ref[t]],
+                    tiles_ref[t],
+                    (((1,), (1,)), ((), ())),
+                    preferred_element_type=F32,
+                )
             )
-            terms.append(jnp.where(t < count, term, 0.0))
-        for i in range(CHUNK):
-            acc_ref[dst_ref[c * CHUNK + i]] += terms[i]
+        for i, t in enumerate(range(c * CHUNK, (c + 1) * CHUNK)):
+            acc_ref[jnp.where(t < count, dst_ref[t], blocks)] += terms[i]
 
     for c in range(tile_total // CHUNK):
         big[c].wait()
@@ -120,6 +119,28 @@
         block = acc_ref[b].astype(BF16)
         for e in range(out_ref.shape[0]):
             out_ref[e, :, b * lanes : (b + 1) * lanes] = block
+
+
+def forward(src, dst, count, near, halo, tiles, cot_full):
+    rows, nodes = near.shape
+    total, lanes, _ = tiles.shape
+    blocks = nodes // lanes
+    dma = pltpu.SemaphoreType.DMA
+    return call(
+        forward_kernel,
+        jax.ShapeDtypeStruct((cot_full.shape[0] // rows, rows, nodes), BF16),
+        [HBM, HBM, HBM, VMEM, VMEM, HBM, ANY],
+        scratch=[
+            pltpu.VMEM((blocks + 1, rows, lanes), F32),
+            pltpu.VMEM((blocks + halo.shape[0], rows, lanes), BF16),
+            pltpu.VMEM((total, lanes, lanes), BF16),
+            pltpu.SMEM((total,), jnp.int32),
+            pltpu.SMEM((total,), jnp.int32),
+            pltpu.SMEM((1,), jnp.int32),
+            dma((3,)),
+            dma((total // CHUNK,)),
+        ],
+    )(src, dst, count, near, halo, tiles, cot_full)
 
 
 def middle_kernel(agg_ref, weight_ref, cot_ref, part_ref, grad_ref, act_ref, pre_ref):
@@ -157,6 +178,7 @@
     rows = grad_ref.shape[0]
     tile_total, lanes, _ = tiles_ref.shape
     blocks = grad_ref.shape[1] // lanes
+    spare = acc_ref.shape[0] - 1
     small = [
         pltpu.make_async_copy(a, b, small_sems.at[i])
         for i, (a, b) in enumerate(((src_hbm, src_ref), (dst_hbm, dst_ref), (count_hbm, count_ref)))
@@ -171,13 +193,13 @@
 
     def chunk(c):
         terms = []
-        for i in range(CHUNK):
-            t = c * CHUNK + i
+        for t in range(c * CHUNK, (c + 1) * CHUNK):
             start = pl.multiple_of(dst_ref[t] * lanes, lanes)
-            term = jnp.dot(grad_ref[:, pl.ds(start, lanes)], tiles_ref[t], preferred_element_type=F32)
-            terms.append(jnp.where(t < count, term, 0.0))
-        for i in range(CHUNK):
-            acc_ref[src_ref[c * CHUNK + i]] += terms[i]
+            terms.append(
+                jnp.dot(grad_ref[:, pl.ds(start, lanes)], tiles_ref[t], preferred_element_type=F32)
+            )
+        for i, t in enumerate(range(c * CHUNK, (c + 1) * CHUNK)):
+            acc_ref[jnp.where(t < count, src_ref[t], spare)] += terms[i]
 
     for c in range(tile_total // CHUNK):
         big[c].wait()
@@ -188,6 +210,33 @@
     for q in range(out_ref.shape[0]):
         out_ref[q, :rows, :] = acc_ref[blocks + q].astype(BF16)
     keep.wait()
+
+
+def backward(src, dst, count, grad, tiles, peers):
+    rows, nodes = grad.shape
+    total, lanes, _ = tiles.shape
+    blocks = nodes // lanes
+    dma = pltpu.SemaphoreType.DMA
+    return call(
+        backward_kernel,
+        (
+            jax.ShapeDtypeStruct((peers, rows + EXTRA, lanes), BF16),
+            jax.ShapeDtypeStruct((blocks, rows, lanes), F32),
+        ),
+        [HBM, HBM, HBM, VMEM, HBM],
+        (VMEM, HBM),
+        scratch=[
+            pltpu.VMEM((blocks + peers + 1, rows, lanes), F32),
+            pltpu.VMEM((total, lanes, lanes), BF16),
+            pltpu.SMEM((total,), jnp.int32),
+            pltpu.SMEM((total,), jnp.int32),
+            pltpu.SMEM((1,), jnp.int32),
+            dma((4,)),
+            dma((total // CHUNK,)),
+        ],
+        flops=200_000_000,
+        nbytes=20_000_000,
+    )(src, dst, count, grad, tiles)
 
 
 def attach_kernel(parts_ref, _, out_ref):
@@ -230,23 +279,14 @@
 
 def shards(features, weight, cotangent, tile_vals, tile_src, tile_dst, tile_count, halo_block):
     rows, nodes = features.shape
-    tiles, lanes, _ = tile_vals.shape
+    lanes = tile_vals.shape[2]
     blocks = nodes // lanes
     peers = lax.axis_size("dom")
     feats = lax.axis_size("feat")
     full = rows * feats
-    chunks = tiles // CHUNK
     shape = jax.ShapeDtypeStruct
     swap = functools.partial(lax.all_to_all, split_axis=0, concat_axis=0, tiled=True)
     dma = pltpu.SemaphoreType.DMA
-    index_scratch = [
-        pltpu.SMEM((tiles,), jnp.int32),
-        pltpu.SMEM((tiles,), jnp.int32),
-        pltpu.SMEM((1,), jnp.int32),
-        dma((4,)),
-        dma((chunks,)),
-    ]
-
     held = functools.partial(pltpu.with_memory_space_constraint, memory_space=pltpu.HBM)
     features, tile_vals, halo_block = held(features), held(tile_vals), held(halo_block)
     tile_src, tile_dst = held(tile_src), held(tile_dst)
@@ -270,17 +310,7 @@
     cotangent, _ = lax.optimization_barrier((cotangent, asked))
     cot_full = lax.all_gather(cotangent, "feat", axis=0, tiled=True)
 
-    spread = call(
-        forward_kernel,
-        shape((feats, rows, nodes), BF16),
-        [HBM, HBM, HBM, HBM, VMEM, HBM, ANY],
-        scratch=[
-            pltpu.VMEM((blocks, rows, lanes), F32),
-            pltpu.VMEM((tiles, lanes, lanes), BF16),
-            pltpu.VMEM((rows, nodes), BF16),
-        ]
-        + index_scratch,
-    )(tile_src, tile_dst, tile_count, features, incoming, tile_vals, cot_full)
+    spread = forward(tile_src, tile_dst, tile_count, near, incoming, tile_vals, cot_full)
     agg = swap(spread, "feat")
 
     part, agg_grad, activated = call(
@@ -298,19 +328,7 @@
     ]
     parts = swap(part, "dom", axis_index_groups=groups)
 
-    outbound, own = call(
-        backward_kernel,
-        (shape((peers, rows + EXTRA, lanes), BF16), shape((blocks, rows, lanes), F32)),
-        [HBM, HBM, HBM, VMEM, HBM],
-        (VMEM, HBM),
-        scratch=[
-            pltpu.VMEM((blocks + peers, rows, lanes), F32),
-            pltpu.VMEM((tiles, lanes, lanes), BF16),
-        ]
-        + index_scratch,
-        flops=200_000_000,
-        nbytes=20_000_000,
-    )(tile_src, tile_dst, tile_count, agg_grad, tile_vals)
+    outbound, own = backward(tile_src, tile_dst, tile_count, agg_grad, tile_vals, peers)
     outbound = call(
         attach_kernel, shape((peers, rows + EXTRA, lanes), BF16), [VMEM, VMEM], aliases={1: 0}
     )(parts, outbound)

time: 112 us -> 110 us (0.982)
  Pallas kernels: 10.5 us -> 8.26 us
    pallas_call x2, Pallas kernels: 6.29 us -> 4.01 us  [the longest x1 2.1 us: forward(): call(forward_kernel, jax.ShapeDtypeStruct((cot_full.shape[0] // rows, row...]
where the time goes in v4:
time: 110 us
  blocking collectives  82.3 us (75%)
  starting transfers between devices  10.6 us (10%)
  Pallas kernels  8.26 us (8%)
  waiting for transfers between devices  7.51 us (7%)
  between operations  1.33 us (1%)
    all_to_all x1, blocking collectives, shards(): returned = swap(outbound, 'dom')  28.3 us
    all_to_all x1, blocking collectives, shards(): asked = swap(request, 'dom')  27.4 us
    all_gather x1, blocking collectives, shards(): cot_full = lax.all_gather(cotangent, 'feat', axis=0, tiled=True)  13.5 us
    all_to_all x1, blocking collectives, shards(): agg = swap(spread, 'feat')  13 us
    all_to_all x1, starting transfers between devices, shards(): incoming = swap(outgoing, 'dom')  5.5 us
    all_to_all x1, starting transfers between devices, shards(): parts = swap(part, 'dom', axis_index_groups=groups)  5.06 us
    all_to_all x1, waiting for transfers between devices, shards(): incoming = swap(outgoing, 'dom')  4.25 us
    all_to_all x1, waiting for transfers between devices, shards(): parts = swap(part, 'dom', axis_index_groups=groups)  3.26 us
  transfers between devices with their start and end apart: 2, of which 2 were waited for; matrix products, arithmetic and copies ran while one was open for 0% of the time, Pallas kernels for 2%

profile of v4, /device:TPU:8, one launch (start us, length us, event | category | flops | bytes accessed | tf_op | source)
XLA Modules:
  0.0 110.0 jit_solution(14047391120552903509)
XLA Ops:
  0.6 0.8 shard_map.103
  1.5 27.4 %all_to_all.25.asked_ref = s32[64,1,128]{2,1,0:T(1,128)S(1)} all-to-all(s32[64,1,128]{2,1,0:T(1,128)S(1)} %get-tuple-element.14), channel_id=1, replica_groups=mesh['dom'=64,'feat'=8] {'dom'}, dimensions={0} | all-to-all | bytes 65536 | tf_op jit(solution)/shard_map/all_to_all | solution.py:301
  28.9 0.9 shard_map.104
  29.8 5.5 %all-to-all-start.1 = ((bf16[64,32,128]{2,1,0:T(8,128)(2,1)}), bf16[64,32,128]{2,1,0:T(8,128)(2,1)S(1)}, u32[]{:S(2)}, u32[]{:S(2)}) async-start(bf16[64,32,128]{2,1,0:T(8,128)(2,1)} %shard_map.104), calls=%async_computation.1 | async-start | bytes 1048576 | tf_op jit(solution)/shard_map/all_to_all | solution.py:309
  36.0 13.5 %all_gather.3._.cot_ref = bf16[256,768]{1,0:T(8,128)(2,1)S(1)} all-gather(bf16[32,768]{1,0:T(8,128)(2,1)} %param.10), channel_id=1, replica_groups=mesh['dom'=64,'feat'=8] {'feat'}, dimensions={0}, use_global_device_ids=true | all-gather | bytes 442368 | tf_op jit(solution)/shard_map/all_gather | solution.py:311
  49.5 0.0 copy-start
  49.5 4.3 %all-to-all-done.1.halo_ref = bf16[64,32,128]{2,1,0:T(8,128)(2,1)S(1)} async-done(((bf16[64,32,128]{2,1,0:T(8,128)(2,1)}), bf16[64,32,128]{2,1,0:T(8,128)(2,1)S(1)}, u32[]{:S(2)}, u32[]{:S(2)}) %all-to-all-start.1) | async-done | bytes 524320 | tf_op jit(solution)/shard_map/all_to_all | solution.py:309
  53.7 2.1 %shard_map.105 = bf16[8,32,768]{2,1,0:T(8,128)(2,1)S(1)} custom-call(s32[70]{0:T(128)} %src_hbm.3, s32[70]{0:T(128)} %dst_hbm.3, s32[1]{0:T(128)S(6)} %copy.13.count_hbm, bf16[32,768]{1,0:T(8,128)(2,1)S(1)} %get-tuple-element.13.feat_ref.near_ref, bf16[64,32,128]{2,1,0:T(8,128)(2,1)S(1)} %all-to-all-done.1.halo_ref, bf16[70,128,128]{2,1,0:T(8,128)(2,1)} %tiles_hbm.3, ...), custom_call_target="tpu_custom_call" | custom-call | flops 1000 | bytes 1000 | tf_op jit(solution)/shard_map/pallas_call | solution.py:129
  55.8 13.0 %all_to_all.26.agg_ref = bf16[8,32,768]{2,1,0:T(8,128)(2,1)S(1)} all-to-all(bf16[8,32,768]{2,1,0:T(8,128)(2,1)S(1)} %shard_map.105), channel_id=1, replica_groups=mesh['dom'=64,'feat'=8] {'feat'}, dimensions={0} | all-to-all | bytes 786432 | tf_op jit(solution)/shard_map/all_to_all | solution.py:314
  68.9 0.0 copy-done
  68.9 1.2 %shard_map.106 = (f32[8,8,128]{2,1,0:T(8,128)}, bf16[32,768]{1,0:T(8,128)(2,1)S(1)}, bf16[32,768]{1,0:T(8,128)(2,1)}) custom-call(bf16[8,32,768]{2,1,0:T(8,128)(2,1)S(1)} %all_to_all.26.agg_ref, bf16[256,256]{1,0:T(8,128)(2,1)S(1)} %copy-done, bf16[256,768]{1,0:T(8,128)(2,1)S(1)} %all_gather.3._.cot_ref), custom_call_target="tpu_custom_call" | custom-call | flops 1000 | bytes 1000 | tf_op jit(solution)/shard_map/pallas_call | solution.py:316
  70.1 5.1 %all-to-all-start.3 = ((f32[8,8,128]{2,1,0:T(8,128)}), f32[8,8,128]{2,1,0:T(8,128)S(1)}, u32[]{:S(2)}, u32[]{:S(2)}) async-start(f32[8,8,128]{2,1,0:T(8,128)} %get-tuple-element.19), calls=%async_computation.3 | async-start | bytes 65536 | tf_op jit(solution)/shard_map/all_to_all | solution.py:329
  75.2 1.9 %shard_map.107 = (bf16[64,40,128]{2,1,0:T(8,128)(2,1)S(1)}, f32[6,32,128]{2,1,0:T(8,128)S(1)}) custom-call(s32[70]{0:T(128)} %src_hbm.3, s32[70]{0:T(128)} %dst_hbm.3, s32[1]{0:T(128)S(6)} %copy.13.count_hbm, bf16[32,768]{1,0:T(8,128)(2,1)S(1)} %get-tuple-element.17.grad_ref, bf16[70,128,128]{2,1,0:T(8,128)(2,1)} %tiles_hbm.3), custom_call_target="tpu_custom_call" | custom-call | flops 200000000 | bytes 20000000 | tf_op jit(solution)/shard_map/pallas_call | solution.py:220
  77.1 3.3 %all-to-all-done.3.parts_ref = f32[8,8,128]{2,1,0:T(8,128)S(1)} async-done(((f32[8,8,128]{2,1,0:T(8,128)}), f32[8,8,128]{2,1,0:T(8,128)S(1)}, u32[]{:S(2)}, u32[]{:S(2)}) %all-to-all-start.3) | async-done | bytes 32800 | tf_op jit(solution)/shard_map/all_to_all | solution.py:329
  80.4 28.3 %all_to_all.27.back_ref = bf16[64,40,128]{2,1,0:T(8,128)(2,1)S(1)} all-to-all(bf16[64,40,128]{2,1,0:T(8,128)(2,1)S(1)} %shard_map.108), channel_id=1, replica_groups=mesh['dom'=64,'feat'=8] {'dom'}, dimensions={0} | all-to-all | bytes 1310720 | tf_op jit(solution)/shard_map/all_to_all | solution.py:335
  108.7 1.3 %shard_map.109 = (bf16[32,768]{1,0:T(8,128)(2,1)}, f32[32,256]{1,0:T(8,128)}) custom-call(s32[64,1,128]{2,1,0:T(1,128)S(1)} %all_to_all.25.asked_ref, f32[6,32,128]{2,1,0:T(8,128)S(1)} %get-tuple-element.18.own_hbm, bf16[64,40,128]{2,1,0:T(8,128)(2,1)S(1)} %all_to_all.27.back_ref), custom_call_target="tpu_custom_call" | custom-call | flops 1000 | bytes 1000 | tf_op jit(solution)/shard_map/pallas_call | solution.py:337
  (1 shorter events, 0.0 us)
Async XLA Ops:
  29.8 23.9 %all-to-all-start.1 = ((bf16[64,32,128]{2,1,0:T(8,128)(2,1)}), bf16[64,32,128]{2,1,0:T(8,128)(2,1)S(1)}, u32[]{:S(2)}, u32[]{:S(2)}) async-start(bf16[64,32,128]{2,1,0:T(8,128)(2,1)} %shard_map.104), calls=%async_computation.1 | async-start | bytes 1048576 | tf_op jit(solution)/shard_map/all_to_all | solution.py:309
  49.5 19.4 %copy-start = (bf16[256,256]{1,0:T(8,128)(2,1)S(1)}, bf16[256,256]{1,0:T(8,128)(2,1)}, u32[]{:S(2)}) copy-start(bf16[256,256]{1,0:T(8,128)(2,1)} %weight_ref.1) | copy-start | bytes 393220
  70.1 10.2 %all-to-all-start.3 = ((f32[8,8,128]{2,1,0:T(8,128)}), f32[8,8,128]{2,1,0:T(8,128)S(1)}, u32[]{:S(2)}, u32[]{:S(2)}) async-start(f32[8,8,128]{2,1,0:T(8,128)} %get-tuple-element.19), calls=%async_computation.3 | async-start | bytes 65536 | tf_op jit(solution)/shard_map/all_to_all | solution.py:329

commit v5 on v4

--- a/solution.py
+++ b/solution.py
@@ -143,7 +143,7 @@
     )(src, dst, count, near, halo, tiles, cot_full)
 
 
-def middle_kernel(agg_ref, weight_ref, cot_ref, part_ref, grad_ref, act_ref, pre_ref):
+def middle_kernel(agg_ref, weight_ref, cot_ref, part_ref, pre_grad_ref, act_ref, pre_ref):
     feats, rows, nodes = agg_ref.shape
     lanes = part_ref.shape[2]
     index = lax.axis_index("feat")
@@ -167,13 +167,13 @@
             ],
             axis=0,
         )
-    grad_ref[...] = jnp.dot(weight_ref[mine, :], grad, preferred_element_type=F32).astype(BF16)
+    pre_grad_ref[...] = grad
     act_ref[...] = jax.nn.silu(pre_ref[mine, :]).astype(BF16)
 
 
 def backward_kernel(
-    src_hbm, dst_hbm, count_hbm, grad_ref, tiles_hbm,
-    out_ref, own_hbm, acc_ref, tiles_ref, src_ref, dst_ref, count_ref, small_sems, sems,
+    src_hbm, dst_hbm, count_hbm, pre_grad_ref, weight_ref, tiles_hbm,
+    out_ref, own_hbm, acc_ref, grad_ref, tiles_ref, src_ref, dst_ref, count_ref, small_sems, sems,
 ):
     rows = grad_ref.shape[0]
     tile_total, lanes, _ = tiles_ref.shape
@@ -186,6 +186,10 @@
     big = tile_copies(tiles_hbm, tiles_ref, sems)
     for copy in small + big:
         copy.start()
+    mine = pl.ds(pl.multiple_of(lax.axis_index("feat") * rows, rows), rows)
+    grad_ref[...] = jnp.dot(
+        weight_ref[mine, :], pre_grad_ref[...], preferred_element_type=F32
+    ).astype(BF16)
     acc_ref[...] = jnp.zeros_like(acc_ref)
     for copy in small:
         copy.wait()
@@ -212,8 +216,8 @@
     keep.wait()
 
 
-def backward(src, dst, count, grad, tiles, peers):
-    rows, nodes = grad.shape
+def backward(src, dst, count, pre_grad, weight, tiles, rows, peers):
+    nodes = pre_grad.shape[1]
     total, lanes, _ = tiles.shape
     blocks = nodes // lanes
     dma = pltpu.SemaphoreType.DMA
@@ -223,10 +227,11 @@
             jax.ShapeDtypeStruct((peers, rows + EXTRA, lanes), BF16),
             jax.ShapeDtypeStruct((blocks, rows, lanes), F32),
         ),
-        [HBM, HBM, HBM, VMEM, HBM],
+        [HBM, HBM, HBM, VMEM, VMEM, HBM],
         (VMEM, HBM),
         scratch=[
             pltpu.VMEM((blocks + peers + 1, rows, lanes), F32),
+            pltpu.VMEM((rows, nodes), BF16),
             pltpu.VMEM((total, lanes, lanes), BF16),
             pltpu.SMEM((total,), jnp.int32),
             pltpu.SMEM((total,), jnp.int32),
@@ -236,7 +241,7 @@
         ],
         flops=200_000_000,
         nbytes=20_000_000,
-    )(src, dst, count, grad, tiles)
+    )(src, dst, count, pre_grad, weight, tiles)
 
 
 def attach_kernel(parts_ref, _, out_ref):
@@ -313,9 +318,9 @@
     spread = forward(tile_src, tile_dst, tile_count, near, incoming, tile_vals, cot_full)
     agg = swap(spread, "feat")
 
-    part, agg_grad, activated = call(
+    part, pre_grad, activated = call(
         middle_kernel,
-        (shape((GROUP, EXTRA, lanes), F32), shape((rows, nodes), BF16), shape((rows, nodes), BF16)),
+        (shape((GROUP, EXTRA, lanes), F32), shape((full, nodes), BF16), shape((rows, nodes), BF16)),
         [VMEM, VMEM, VMEM],
         (VMEM, VMEM, VMEM),
         scratch=[pltpu.VMEM((full, nodes), F32)],
@@ -328,7 +333,9 @@
     ]
     parts = swap(part, "dom", axis_index_groups=groups)
 
-    outbound, own = backward(tile_src, tile_dst, tile_count, agg_grad, tile_vals, peers)
+    outbound, own = backward(
+        tile_src, tile_dst, tile_count, pre_grad, weight, tile_vals, rows, peers
+    )
     outbound = call(
         attach_kernel, shape((peers, rows + EXTRA, lanes), BF16), [VMEM, VMEM], aliases={1: 0}
     )(parts, outbound)

time: 110 us -> 111 us (level)
  Pallas kernels: 8.26 us -> 9.41 us
where the time goes in v5:
time: 111 us
  blocking collectives  83 us (75%)
  starting transfers between devices  9.84 us (9%)
  Pallas kernels  9.41 us (8%)
  waiting for transfers between devices  7.07 us (6%)
  between operations  1.33 us (1%)
    all_to_all x1, blocking collectives, shards(): returned = swap(outbound, 'dom')  29 us
    all_to_all x1, blocking collectives, shards(): asked = swap(request, 'dom')  27.4 us
    all_gather x1, blocking collectives, shards(): cot_full = lax.all_gather(cotangent, 'feat', axis=0, tiled=True)  13.5 us
    all_to_all x1, blocking collectives, shards(): agg = swap(spread, 'feat')  13 us
    all_to_all x1, starting transfers between devices, shards(): incoming = swap(outgoing, 'dom')  5.5 us
    all_to_all x1, starting transfers between devices, shards(): parts = swap(part, 'dom', axis_index_groups=groups)  4.34 us
    all_to_all x1, waiting for transfers between devices, shards(): incoming = swap(outgoing, 'dom')  4.25 us
    pallas_call x1, Pallas kernels, forward(): call(forward_kernel, jax.ShapeDtypeStruct((cot_full.shape[0] // rows, row...  2.83 us
  transfers between devices with their start and end apart: 2, of which 2 were waited for; matrix products, arithmetic and copies ran while one was open for 0% of the time, Pallas kernels for 2%

profile of v5, /device:TPU:8, one launch (start us, length us, event | category | flops | bytes accessed | tf_op | source)
XLA Modules:
  0.0 110.7 jit_solution(6032608500810397530)
XLA Ops:
  0.6 0.8 shard_map.103
  1.5 27.4 %all_to_all.25.asked_ref = s32[64,1,128]{2,1,0:T(1,128)S(1)} all-to-all(s32[64,1,128]{2,1,0:T(1,128)S(1)} %get-tuple-element.14), channel_id=1, replica_groups=mesh['dom'=64,'feat'=8] {'dom'}, dimensions={0} | all-to-all | bytes 65536 | tf_op jit(solution)/shard_map/all_to_all | solution.py:306
  28.9 0.9 shard_map.104
  29.8 5.5 %all-to-all-start.1 = ((bf16[64,32,128]{2,1,0:T(8,128)(2,1)}), bf16[64,32,128]{2,1,0:T(8,128)(2,1)S(1)}, u32[]{:S(2)}, u32[]{:S(2)}) async-start(bf16[64,32,128]{2,1,0:T(8,128)(2,1)} %shard_map.104), calls=%async_computation.1 | async-start | bytes 1048576 | tf_op jit(solution)/shard_map/all_to_all | solution.py:314
  36.0 13.5 %all_gather.3._.cot_ref = bf16[256,768]{1,0:T(8,128)(2,1)S(1)} all-gather(bf16[32,768]{1,0:T(8,128)(2,1)} %param.10), channel_id=1, replica_groups=mesh['dom'=64,'feat'=8] {'feat'}, dimensions={0}, use_global_device_ids=true | all-gather | bytes 442368 | tf_op jit(solution)/shard_map/all_gather | solution.py:316
  49.5 0.0 copy-start
  49.5 4.3 %all-to-all-done.1.halo_ref = bf16[64,32,128]{2,1,0:T(8,128)(2,1)S(1)} async-done(((bf16[64,32,128]{2,1,0:T(8,128)(2,1)}), bf16[64,32,128]{2,1,0:T(8,128)(2,1)S(1)}, u32[]{:S(2)}, u32[]{:S(2)}) %all-to-all-start.1) | async-done | bytes 524320 | tf_op jit(solution)/shard_map/all_to_all | solution.py:314
  53.7 2.8 %shard_map.105 = bf16[8,32,768]{2,1,0:T(8,128)(2,1)S(1)} custom-call(s32[70]{0:T(128)} %src_hbm.3, s32[70]{0:T(128)} %dst_hbm.3, s32[1]{0:T(128)S(6)} %copy.13.count_hbm, bf16[32,768]{1,0:T(8,128)(2,1)S(1)} %get-tuple-element.13.feat_ref.near_ref, bf16[64,32,128]{2,1,0:T(8,128)(2,1)S(1)} %all-to-all-done.1.halo_ref, bf16[70,128,128]{2,1,0:T(8,128)(2,1)} %tiles_hbm.3, ...), custom_call_target="tpu_custom_call" | custom-call | flops 1000 | bytes 1000 | tf_op jit(solution)/shard_map/pallas_call | solution.py:129
  56.6 13.0 %all_to_all.26.agg_ref = bf16[8,32,768]{2,1,0:T(8,128)(2,1)S(1)} all-to-all(bf16[8,32,768]{2,1,0:T(8,128)(2,1)S(1)} %shard_map.105), channel_id=1, replica_groups=mesh['dom'=64,'feat'=8] {'feat'}, dimensions={0} | all-to-all | bytes 786432 | tf_op jit(solution)/shard_map/all_to_all | solution.py:319
  69.6 0.0 copy-done
  69.6 1.2 %shard_map.106 = (f32[8,8,128]{2,1,0:T(8,128)}, bf16[256,768]{1,0:T(8,128)(2,1)S(1)}, bf16[32,768]{1,0:T(8,128)(2,1)}) custom-call(bf16[8,32,768]{2,1,0:T(8,128)(2,1)S(1)} %all_to_all.26.agg_ref, bf16[256,256]{1,0:T(8,128)(2,1)S(1)} %copy-done, bf16[256,768]{1,0:T(8,128)(2,1)S(1)} %all_gather.3._.cot_ref), custom_call_target="tpu_custom_call" | custom-call | flops 1000 | bytes 1000 | tf_op jit(solution)/shard_map/pallas_call | solution.py:321
  70.8 4.3 %all-to-all-start.3 = ((f32[8,8,128]{2,1,0:T(8,128)}), f32[8,8,128]{2,1,0:T(8,128)S(1)}, u32[]{:S(2)}, u32[]{:S(2)}) async-start(f32[8,8,128]{2,1,0:T(8,128)} %get-tuple-element.19), calls=%async_computation.3 | async-start | bytes 65536 | tf_op jit(solution)/shard_map/all_to_all | solution.py:334
  75.2 2.4 %shard_map.107 = (bf16[64,40,128]{2,1,0:T(8,128)(2,1)S(1)}, f32[6,32,128]{2,1,0:T(8,128)S(1)}) custom-call(s32[70]{0:T(128)} %src_hbm.3, s32[70]{0:T(128)} %dst_hbm.3, s32[1]{0:T(128)S(6)} %copy.13.count_hbm, bf16[256,768]{1,0:T(8,128)(2,1)S(1)} %get-tuple-element.17.pre_grad_ref, bf16[256,256]{1,0:T(8,128)(2,1)S(1)} %copy-done, bf16[70,128,128]{2,1,0:T(8,128)(2,1)} %tiles_hbm.3), custom_call_target="tpu_custom_call" | custom-call | flops 200000000 | bytes 20000000 | tf_op jit(solution)/shard_map/pallas_call | solution.py:224
  77.5 2.8 %all-to-all-done.3.parts_ref = f32[8,8,128]{2,1,0:T(8,128)S(1)} async-done(((f32[8,8,128]{2,1,0:T(8,128)}), f32[8,8,128]{2,1,0:T(8,128)S(1)}, u32[]{:S(2)}, u32[]{:S(2)}) %all-to-all-start.3) | async-done | bytes 32800 | tf_op jit(solution)/shard_map/all_to_all | solution.py:334
  80.4 29.0 %all_to_all.27.back_ref = bf16[64,40,128]{2,1,0:T(8,128)(2,1)S(1)} all-to-all(bf16[64,40,128]{2,1,0:T(8,128)(2,1)S(1)} %shard_map.108), channel_id=1, replica_groups=mesh['dom'=64,'feat'=8] {'dom'}, dimensions={0} | all-to-all | bytes 1310720 | tf_op jit(solution)/shard_map/all_to_all | solution.py:342
  109.4 1.3 %shard_map.109 = (bf16[32,768]{1,0:T(8,128)(2,1)}, f32[32,256]{1,0:T(8,128)}) custom-call(s32[64,1,128]{2,1,0:T(1,128)S(1)} %all_to_all.25.asked_ref, f32[6,32,128]{2,1,0:T(8,128)S(1)} %get-tuple-element.18.own_hbm, bf16[64,40,128]{2,1,0:T(8,128)(2,1)S(1)} %all_to_all.27.back_ref), custom_call_target="tpu_custom_call" | custom-call | flops 1000 | bytes 1000 | tf_op jit(solution)/shard_map/pallas_call | solution.py:344
  (1 shorter events, 0.0 us)
Async XLA Ops:
  29.8 23.9 %all-to-all-start.1 = ((bf16[64,32,128]{2,1,0:T(8,128)(2,1)}), bf16[64,32,128]{2,1,0:T(8,128)(2,1)S(1)}, u32[]{:S(2)}, u32[]{:S(2)}) async-start(bf16[64,32,128]{2,1,0:T(8,128)(2,1)} %shard_map.104), calls=%async_computation.1 | async-start | bytes 1048576 | tf_op jit(solution)/shard_map/all_to_all | solution.py:314
  49.5 20.1 %copy-start = (bf16[256,256]{1,0:T(8,128)(2,1)S(1)}, bf16[256,256]{1,0:T(8,128)(2,1)}, u32[]{:S(2)}) copy-start(bf16[256,256]{1,0:T(8,128)(2,1)} %weight_ref.3) | copy-start | bytes 393220
  70.8 9.5 %all-to-all-start.3 = ((f32[8,8,128]{2,1,0:T(8,128)}), f32[8,8,128]{2,1,0:T(8,128)S(1)}, u32[]{:S(2)}, u32[]{:S(2)}) async-start(f32[8,8,128]{2,1,0:T(8,128)} %get-tuple-element.19), calls=%async_computation.3 | async-start | bytes 65536 | tf_op jit(solution)/shard_map/all_to_all | solution.py:334

commit v6 on v5

--- a/solution.py
+++ b/solution.py
@@ -143,16 +143,14 @@
     )(src, dst, count, near, halo, tiles, cot_full)
 
 
-def middle_kernel(agg_ref, weight_ref, cot_ref, part_ref, pre_grad_ref, act_ref, pre_ref):
+def middle_kernel(agg_ref, weight_ref, cot_ref, part_ref, pre_grad_ref):
     feats, rows, nodes = agg_ref.shape
     lanes = part_ref.shape[2]
     index = lax.axis_index("feat")
-    mine = pl.ds(pl.multiple_of(index * rows, rows), rows)
     agg = agg_ref[...].reshape(feats * rows, nodes)
     pre = lax.dot_general(
         weight_ref[...], agg, (((0,), (0,)), ((), ())), preferred_element_type=F32
     )
-    pre_ref[...] = pre
     sig = jax.nn.sigmoid(pre)
     grad = (cot_ref[...].astype(F32) * sig * (1.0 + pre * (1.0 - sig))).astype(BF16)
     part = lax.dot_general(
@@ -168,14 +166,13 @@
             axis=0,
         )
     pre_grad_ref[...] = grad
-    act_ref[...] = jax.nn.silu(pre_ref[mine, :]).astype(BF16)
 
 
 def backward_kernel(
-    src_hbm, dst_hbm, count_hbm, pre_grad_ref, weight_ref, tiles_hbm,
-    out_ref, own_hbm, acc_ref, grad_ref, tiles_ref, src_ref, dst_ref, count_ref, small_sems, sems,
+    src_hbm, dst_hbm, count_hbm, pre_grad_ref, weight_ref, agg_ref, tiles_hbm,
+    out_ref, own_hbm, act_ref, acc_ref, grad_ref, pre_ref, tiles_ref, src_ref, dst_ref, count_ref, small_sems, sems,
 ):
-    rows = grad_ref.shape[0]
+    rows, nodes = grad_ref.shape
     tile_total, lanes, _ = tiles_ref.shape
     blocks = grad_ref.shape[1] // lanes
     spare = acc_ref.shape[0] - 1
@@ -213,11 +210,18 @@
     keep.start()
     for q in range(out_ref.shape[0]):
         out_ref[q, :rows, :] = acc_ref[blocks + q].astype(BF16)
+    pre_ref[...] = lax.dot_general(
+        weight_ref[...],
+        agg_ref[...].reshape(-1, nodes),
+        (((0,), (0,)), ((), ())),
+        preferred_element_type=F32,
+    )
+    act_ref[...] = jax.nn.silu(pre_ref[mine, :]).astype(BF16)
     keep.wait()
 
 
-def backward(src, dst, count, pre_grad, weight, tiles, rows, peers):
-    nodes = pre_grad.shape[1]
+def backward(src, dst, count, pre_grad, weight, agg, tiles, peers):
+    _, rows, nodes = agg.shape
     total, lanes, _ = tiles.shape
     blocks = nodes // lanes
     dma = pltpu.SemaphoreType.DMA
@@ -226,12 +230,14 @@
         (
             jax.ShapeDtypeStruct((peers, rows + EXTRA, lanes), BF16),
             jax.ShapeDtypeStruct((blocks, rows, lanes), F32),
+            jax.ShapeDtypeStruct((rows, nodes), BF16),
         ),
-        [HBM, HBM, HBM, VMEM, VMEM, HBM],
-        (VMEM, HBM),
+        [HBM, HBM, HBM, VMEM, VMEM, VMEM, HBM],
+        (VMEM, HBM, VMEM),
         scratch=[
             pltpu.VMEM((blocks + peers + 1, rows, lanes), F32),
             pltpu.VMEM((rows, nodes), BF16),
+            pltpu.VMEM(pre_grad.shape, F32),
             pltpu.VMEM((total, lanes, lanes), BF16),
             pltpu.SMEM((total,), jnp.int32),
             pltpu.SMEM((total,), jnp.int32),
@@ -241,7 +247,7 @@
         ],
         flops=200_000_000,
         nbytes=20_000_000,
-    )(src, dst, count, pre_grad, weight, tiles)
+    )(src, dst, count, pre_grad, weight, agg, tiles)
 
 
 def attach_kernel(parts_ref, _, out_ref):
@@ -318,12 +324,11 @@
     spread = forward(tile_src, tile_dst, tile_count, near, incoming, tile_vals, cot_full)
     agg = swap(spread, "feat")
 
-    part, pre_grad, activated = call(
+    part, pre_grad = call(
         middle_kernel,
-        (shape((GROUP, EXTRA, lanes), F32), shape((full, nodes), BF16), shape((rows, nodes), BF16)),
+        (shape((GROUP, EXTRA, lanes), F32), shape((full, nodes), BF16)),
         [VMEM, VMEM, VMEM],
-        (VMEM, VMEM, VMEM),
-        scratch=[pltpu.VMEM((full, nodes), F32)],
+        (VMEM, VMEM),
     )(agg, weight, cot_full)
 
     groups = [
@@ -333,8 +338,8 @@
     ]
     parts = swap(part, "dom", axis_index_groups=groups)
 
-    outbound, own = backward(
-        tile_src, tile_dst, tile_count, pre_grad, weight, tile_vals, rows, peers
+    outbound, own, activated = backward(
+        tile_src, tile_dst, tile_count, pre_grad, weight, agg, tile_vals, peers
     )
     outbound = call(
         attach_kernel, shape((peers, rows + EXTRA, lanes), BF16), [VMEM, VMEM], aliases={1: 0}

time: 111 us -> 111 us (level)
  transfers between devices with their start and end apart: 2 -> 2, of which waited for: 2 -> 2; matrix products, arithmetic and copies ran while one was open for 0% -> 0% of each run, Pallas kernels for 2% -> 3%
where the time goes in v6:
time: 111 us
  blocking collectives  83.2 us (75%)
  Pallas kernels  10.3 us (9%)
  starting transfers between devices  9.66 us (9%)
  waiting for transfers between devices  6.13 us (6%)
  between operations  1.33 us (1%)
    all_to_all x1, blocking collectives, shards(): returned = swap(outbound, 'dom')  29.2 us
    all_to_all x1, blocking collectives, shards(): asked = swap(request, 'dom')  27.4 us
    all_gather x1, blocking collectives, shards(): cot_full = lax.all_gather(cotangent, 'feat', axis=0, tiled=True)  13.5 us
    all_to_all x1, blocking collectives, shards(): agg = swap(spread, 'feat')  13 us
    all_to_all x1, starting transfers between devices, shards(): incoming = swap(outgoing, 'dom')  5.5 us
    all_to_all x1, waiting for transfers between devices, shards(): incoming = swap(outgoing, 'dom')  4.25 us
    all_to_all x1, starting transfers between devices, shards(): parts = swap(part, 'dom', axis_index_groups=groups)  4.16 us
    pallas_call x1, Pallas kernels, backward(): call(backward_kernel, (jax.ShapeDtypeStruct((peers, rows + EXTRA, lanes),...  3.3 us
  transfers between devices with their start and end apart: 2, of which 2 were waited for; matrix products, arithmetic and copies ran while one was open for 0% of the time, Pallas kernels for 3%

profile of v6, /device:TPU:8, one launch (start us, length us, event | category | flops | bytes accessed | tf_op | source)
XLA Modules:
  0.0 110.7 jit_solution(12947119516825272697)
XLA Ops:
  0.6 0.8 shard_map.103
  1.5 27.4 %all_to_all.25.asked_ref = s32[64,1,128]{2,1,0:T(1,128)S(1)} all-to-all(s32[64,1,128]{2,1,0:T(1,128)S(1)} %get-tuple-element.14), channel_id=1, replica_groups=mesh['dom'=64,'feat'=8] {'dom'}, dimensions={0} | all-to-all | bytes 65536 | tf_op jit(solution)/shard_map/all_to_all | solution.py:312
  28.9 0.9 shard_map.104
  29.8 5.5 %all-to-all-start.1 = ((bf16[64,32,128]{2,1,0:T(8,128)(2,1)}), bf16[64,32,128]{2,1,0:T(8,128)(2,1)S(1)}, u32[]{:S(2)}, u32[]{:S(2)}) async-start(bf16[64,32,128]{2,1,0:T(8,128)(2,1)} %shard_map.104), calls=%async_computation.1 | async-start | bytes 1048576 | tf_op jit(solution)/shard_map/all_to_all | solution.py:320
  36.0 13.5 %all_gather.3._.cot_ref = bf16[256,768]{1,0:T(8,128)(2,1)S(1)} all-gather(bf16[32,768]{1,0:T(8,128)(2,1)} %param.10), channel_id=1, replica_groups=mesh['dom'=64,'feat'=8] {'feat'}, dimensions={0}, use_global_device_ids=true | all-gather | bytes 442368 | tf_op jit(solution)/shard_map/all_gather | solution.py:322
  49.5 0.0 copy-start
  49.5 4.3 %all-to-all-done.1.halo_ref = bf16[64,32,128]{2,1,0:T(8,128)(2,1)S(1)} async-done(((bf16[64,32,128]{2,1,0:T(8,128)(2,1)}), bf16[64,32,128]{2,1,0:T(8,128)(2,1)S(1)}, u32[]{:S(2)}, u32[]{:S(2)}) %all-to-all-start.1) | async-done | bytes 524320 | tf_op jit(solution)/shard_map/all_to_all | solution.py:320
  53.7 2.8 %shard_map.105 = bf16[8,32,768]{2,1,0:T(8,128)(2,1)S(1)} custom-call(s32[70]{0:T(128)} %src_hbm.3, s32[70]{0:T(128)} %dst_hbm.3, s32[1]{0:T(128)S(6)} %copy.13.count_hbm, bf16[32,768]{1,0:T(8,128)(2,1)S(1)} %get-tuple-element.13.feat_ref.near_ref, bf16[64,32,128]{2,1,0:T(8,128)(2,1)S(1)} %all-to-all-done.1.halo_ref, bf16[70,128,128]{2,1,0:T(8,128)(2,1)} %tiles_hbm.3, ...), custom_call_target="tpu_custom_call" | custom-call | flops 1000 | bytes 1000 | tf_op jit(solution)/shard_map/pallas_call | solution.py:129
  56.6 13.0 %all_to_all.26.agg_ref = bf16[8,32,768]{2,1,0:T(8,128)(2,1)S(1)} all-to-all(bf16[8,32,768]{2,1,0:T(8,128)(2,1)S(1)} %shard_map.105), channel_id=1, replica_groups=mesh['dom'=64,'feat'=8] {'feat'}, dimensions={0} | all-to-all | bytes 786432 | tf_op jit(solution)/shard_map/all_to_all | solution.py:325
  69.6 0.0 copy-done
  69.6 1.2 %shard_map.106 = (f32[8,8,128]{2,1,0:T(8,128)}, bf16[256,768]{1,0:T(8,128)(2,1)S(1)}) custom-call(bf16[8,32,768]{2,1,0:T(8,128)(2,1)S(1)} %all_to_all.26.agg_ref, bf16[256,256]{1,0:T(8,128)(2,1)S(1)} %copy-done, bf16[256,768]{1,0:T(8,128)(2,1)S(1)} %all_gather.3._.cot_ref), custom_call_target="tpu_custom_call" | custom-call | flops 1000 | bytes 1000 | tf_op jit(solution)/shard_map/pallas_call | solution.py:327
  70.8 4.2 %all-to-all-start.3 = ((f32[8,8,128]{2,1,0:T(8,128)}), f32[8,8,128]{2,1,0:T(8,128)S(1)}, u32[]{:S(2)}, u32[]{:S(2)}) async-start(f32[8,8,128]{2,1,0:T(8,128)} %get-tuple-element.19), calls=%async_computation.3 | async-start | bytes 65536 | tf_op jit(solution)/shard_map/all_to_all | solution.py:339
  75.0 3.3 %shard_map.107 = (bf16[64,40,128]{2,1,0:T(8,128)(2,1)S(1)}, f32[6,32,128]{2,1,0:T(8,128)S(1)}, bf16[32,768]{1,0:T(8,128)(2,1)}) custom-call(s32[70]{0:T(128)} %src_hbm.3, s32[70]{0:T(128)} %dst_hbm.3, s32[1]{0:T(128)S(6)} %copy.13.count_hbm, bf16[256,768]{1,0:T(8,128)(2,1)S(1)} %get-tuple-element.16.pre_grad_ref, bf16[256,256]{1,0:T(8,128)(2,1)S(1)} %copy-done, ...), custom_call_target="tpu_custom_call" | custom-call | flops 200000000 | bytes 20000000 | tf_op jit(solution)/shard_map/pallas_call | solution.py:228
  78.3 1.9 %all-to-all-done.3.parts_ref = f32[8,8,128]{2,1,0:T(8,128)S(1)} async-done(((f32[8,8,128]{2,1,0:T(8,128)}), f32[8,8,128]{2,1,0:T(8,128)S(1)}, u32[]{:S(2)}, u32[]{:S(2)}) %all-to-all-start.3) | async-done | bytes 32800 | tf_op jit(solution)/shard_map/all_to_all | solution.py:339
  80.2 29.2 %all_to_all.27.back_ref = bf16[64,40,128]{2,1,0:T(8,128)(2,1)S(1)} all-to-all(bf16[64,40,128]{2,1,0:T(8,128)(2,1)S(1)} %shard_map.108), channel_id=1, replica_groups=mesh['dom'=64,'feat'=8] {'dom'}, dimensions={0} | all-to-all | bytes 1310720 | tf_op jit(solution)/shard_map/all_to_all | solution.py:347
  109.4 1.3 %shard_map.109 = (bf16[32,768]{1,0:T(8,128)(2,1)}, f32[32,256]{1,0:T(8,128)}) custom-call(s32[64,1,128]{2,1,0:T(1,128)S(1)} %all_to_all.25.asked_ref, f32[6,32,128]{2,1,0:T(8,128)S(1)} %get-tuple-element.18.own_hbm, bf16[64,40,128]{2,1,0:T(8,128)(2,1)S(1)} %all_to_all.27.back_ref), custom_call_target="tpu_custom_call" | custom-call | flops 1000 | bytes 1000 | tf_op jit(solution)/shard_map/pallas_call | solution.py:349
  (1 shorter events, 0.0 us)
Async XLA Ops:
  29.8 23.9 %all-to-all-start.1 = ((bf16[64,32,128]{2,1,0:T(8,128)(2,1)}), bf16[64,32,128]{2,1,0:T(8,128)(2,1)S(1)}, u32[]{:S(2)}, u32[]{:S(2)}) async-start(bf16[64,32,128]{2,1,0:T(8,128)(2,1)} %shard_map.104), calls=%async_computation.1 | async-start | bytes 1048576 | tf_op jit(solution)/shard_map/all_to_all | solution.py:320
  49.5 20.1 %copy-start = (bf16[256,256]{1,0:T(8,128)(2,1)S(1)}, bf16[256,256]{1,0:T(8,128)(2,1)}, u32[]{:S(2)}) copy-start(bf16[256,256]{1,0:T(8,128)(2,1)} %weight_ref.3) | copy-start | bytes 393220
  70.8 9.3 %all-to-all-start.3 = ((f32[8,8,128]{2,1,0:T(8,128)}), f32[8,8,128]{2,1,0:T(8,128)S(1)}, u32[]{:S(2)}, u32[]{:S(2)}) async-start(f32[8,8,128]{2,1,0:T(8,128)} %get-tuple-element.19), calls=%async_computation.3 | async-start | bytes 65536 | tf_op jit(solution)/shard_map/all_to_all | solution.py:339
